TPU v7x, 256 devices: a whole 4x4x8 slice. The times are simulated.
256 devices in a mesh: section: 2 (over z_lo), img: 16 (over x, z_hi), ch: 8 (over y, core).
Axes of the slice: x: 4, y: 4, z: 8 (z_hi: 4, z_lo: 2; z = z_hi * 2 + z_lo), core: 2. Of those that a mesh axis runs over, the one named last changes fastest.
Arguments:
- pixels: bfloat16 [32, 64, 28, 640], P('img', 'ch'), may hold values from -6 to 6
- first_gain: float32 [640], replicated, may hold values from 0.25 to 1.75
- first_shift: float32 [640], replicated, may hold values from -3 to 3
- first_kernel: bfloat16 [3, 3, 640, 640], P(None, None, 'img'), may hold values from -0.078125 to 0.078125
- projection: bfloat16 [640, 2560], P('img'), may hold values from -0.25 to 0.25
- second_gain: float32 [2560], replicated, may hold values from 0.25 to 1.75
- second_shift: float32 [2560], replicated, may hold values from -3 to 3
- second_kernel: bfloat16 [3, 3, 2560, 2560], P(None, None, ('img', 'ch')), may hold values from -0.0390625 to 0.0390625
Outputs:
- section_outputs: bfloat16 [2, 32, 32, 14, 2560], P('section', 'img', 'ch')
All inputs are finite; a program needn't handle non-finite values.
Results may differ from a plain program's by a relative error of at most 0.013.
Values may be sent and summed in bfloat16 or wider, within the bound.
A program may use at most 128 MiB of HBM per device.

v0:
```python
import jax
import jax.numpy as jnp
from jax import lax
from jax.sharding import PartitionSpec as P

LAYOUT = ("NHWC", "HWIO", "NHWC")


def extended(cells, sides, width):
    for axis, dim in sides:
        count = lax.axis_size(axis)
        ends = count - 1
        head = lax.slice_in_dim(cells, 0, width, axis=dim)
        tail = lax.slice_in_dim(cells, cells.shape[dim] - width, cells.shape[dim], axis=dim)
        cells = jnp.concatenate(
            [
                lax.ppermute(tail, axis, [(i, (i + 1) % count) for i in range(ends)]),
                cells,
                lax.ppermute(head, axis, [((i + 1) % count, i) for i in range(ends)]),
            ],
            axis=dim,
        )
    return cells


def from_behind(array, axis, by):
    count = lax.axis_size(axis)
    pairs = [(i, i + by) for i in range(count) if 0 <= i + by < count]
    return lax.ppermute(array, axis, pairs)


def convolve(inputs, kernel, padding):
    return lax.conv_general_dilated(
        inputs,
        kernel,
        (1, 1),
        padding,
        dimension_numbers=LAYOUT,
        preferred_element_type=jnp.float32,
    )


def reduce_resolution(value_entries):
    count, height, breadth, depth = value_entries.shape
    blocks = value_entries.reshape(count, height // 2, 2, breadth // 2, 2, depth)
    return jnp.sum(blocks, axis=(2, 4)) * 0.25


def pick_group(value_entries, groups, shards, member):
    lead = value_entries.shape[:-1]
    per_block = value_entries.shape[-1] // (groups * shards)
    split = value_entries.reshape(lead + (groups, shards, per_block))
    chosen = lax.dynamic_slice_in_dim(split, member, 1, len(lead) + 1)
    return chosen.reshape(lead + (groups * per_block,))


def arrange_groups(value_entries, groups, shards):
    lead = value_entries.shape[:-1]
    per_block = value_entries.shape[-1] // (groups * shards)
    split = value_entries.reshape(lead + (groups, shards, per_block))
    swapped = jnp.swapaxes(split, len(lead), len(lead) + 1)
    return swapped.reshape(lead + (groups * shards * per_block,))


def body(
    pixels,
    first_gain,
    first_shift,
    first_kernel,
    projection,
    second_gain,
    second_shift,
    second_kernel,
):
    section_id = lax.axis_index("section")
    is_first = section_id == 0
    is_second = section_id == 1
    groups = lax.axis_size("img")
    shards = lax.axis_size("ch")
    member = lax.axis_index("ch")
    images, rows, columns, depth = pixels.shape
    out_rows = rows // 2
    out_cols = columns // 2
    wide = second_gain.shape[0]
    normalized_input = jax.nn.relu(pixels.astype(jnp.float32) * first_gain + first_shift).astype(
        jnp.bfloat16
    )
    padded = extended(normalized_input, (("ch", 1),), 1)
    initial_blank = jnp.zeros((images, rows, columns, depth), jnp.float32)
    piece = lax.all_gather(first_kernel, "img", axis=2, tiled=True)

    def first_compute():
        return initial_blank + convolve(padded, piece, ((0, 0), (1, 1)))

    convolved = lax.cond(is_first, first_compute, lambda: initial_blank)
    blended_result = convolved + pixels.astype(jnp.float32)
    averaged_pixels = reduce_resolution(blended_result).astype(jnp.bfloat16)
    all_rows = out_rows * shards
    flat_pooled = averaged_pixels.reshape(images * out_rows * out_cols, depth)

    def project_piece(total, piece):

        def project_compute():
            return jnp.dot(flat_pooled, piece, preferred_element_type=jnp.float32)

        return lax.cond(is_first, project_compute, lambda: total)

    proj_empty = jnp.zeros((flat_pooled.shape[0], wide), jnp.float32)
    summed_proj = project_piece(proj_empty, lax.all_gather(projection, "img", axis=0, tiled=True))
    own_rows = summed_proj.astype(jnp.bfloat16).reshape(images, out_rows, out_cols, wide)
    arrived = from_behind(own_rows, "section", 1)
    sorted_layout = arrange_groups(arrived, groups, shards)
    channel_in = lax.all_to_all(sorted_layout, "ch", split_axis=3, concat_axis=1, tiled=True)
    gain_part = pick_group(second_gain, groups, shards, member)
    shift_part = pick_group(second_shift, groups, shards, member)
    second_in = jax.nn.relu(channel_in.astype(jnp.float32) * gain_part + shift_part).astype(
        jnp.bfloat16
    )

    def second_piece(total, piece):

        def second_compute():
            return total + convolve(second_in, piece, ((1, 1), (1, 1)))

        return lax.cond(is_second, second_compute, lambda: total)

    second_empty = jnp.zeros((images, all_rows, out_cols, wide), jnp.float32)
    partial_value = second_piece(
        second_empty, lax.all_gather(second_kernel, "img", axis=2, tiled=True)
    )
    summed = lax.psum_scatter(
        partial_value.astype(jnp.bfloat16), "ch", scatter_dimension=1, tiled=True
    ).astype(jnp.float32)
    block = (summed + arrived.astype(jnp.float32)).astype(jnp.bfloat16)
    final = jnp.where(is_first, own_rows, block)
    return final[None]


def solution(mesh):
    placed = (
        P("img", "ch", None, None),
        P(),
        P(),
        P(None, None, "img", None),
        P("img", None),
        P(),
        P(),
        P(None, None, ("img", "ch"), None),
    )
    return jax.shard_map(
        body,
        mesh=mesh,
        in_specs=placed,
        out_specs=P("section", "img", "ch", None, None),
        check_vma=False,
    )
```

profile of v0, /device:TPU:59, one launch (start us, length us, event | category | flops | bytes accessed | tf_op | source)
XLA Modules:
  0.0 538.5 jit_solution(9953373410711621060)
XLA Ops:
  6.5 0.7 all-gather.4.cloned.1.call-update
  7.3 0.7 all-gather.6.cloned.1.call-update
  8.1 3.0 copy.92
  11.5 1.3 collective-permute-start
  12.8 3.2 collective-permute-start.1
  16.0 1.0 collective-permute-done.1
  17.0 0.7 pad_maximum_fusion
  17.7 101.6 %all-gather.4.cloned.1.call-done = bf16[3,3,640,640]{3,2,1,0:T(8,128)(2,1)} async-done(((bf16[3,3,40,640]{3,2,1,0:T(8,128)(2,1)}), bf16[3,3,640,640]{3,2,1,0:T(8,128)(2,1)}) %all-gather.4.cloned.1.call-update) | async-done | bytes 7372816 | tf_op jit(solution)/shard_map/all_gather | solution.py:90
  119.5 0.9 copy.85
  120.3 0.6 reduce_sum.9
  121.1 66.0 %all-gather.6.cloned.1.call-done = bf16[640,2560]{1,0:T(8,128)(2,1)} async-done(((bf16[40,2560]{1,0:T(8,128)(2,1)}), bf16[640,2560]{1,0:T(8,128)(2,1)}) %all-gather.6.cloned.1.call-update) | async-done | bytes 3276816 | tf_op jit(solution)/shard_map/all_gather | solution.py:109
  187.2 1.5 collective-permute-start.2
  188.7 19.1 %collective-permute-done.2 = bf16[2,4,14,2560]{3,1,2,0:T(4,128)(2,1)S(1)} collective-permute-done((bf16[2,4,14,2560]{3,1,2,0:T(4,128)(2,1)S(1)}, bf16[2,4,14,2560]{3,1,2,0:T(4,128)(2,1)S(1)}, u32[]{:S(2)}, u32[]{:S(2)}) %collective-permute-start.2) | collective-permute-done | bytes 573472 | tf_op jit(solution)/shard_map/ppermute | solution.py:29
  207.8 9.6 %reshape.36 = bf16[2,4,14,16,8,20]{5,4,3,1,2,0:T(8,128)(2,1)} reshape(bf16[2,4,14,2560]{3,1,2,0:T(4,128)(2,1)S(1)} %collective-permute-done.2) | data formatting | bytes 1146880 | tf_op jit(solution)/shard_map/reshape | solution.py:60
  217.4 12.8 %copy.96 = bf16[2,4,14,8,16,20]{2,1,0,5,4,3:T(4,128)(2,1)} copy(bf16[2,4,14,8,16,20]{5,3,4,1,2,0:T(8,128)(2,1)} %bitcast.56) | data formatting | bytes 1146880 | tf_op jit(solution)/shard_map/reshape | solution.py:62
  230.2 10.2 %reshape.77 = bf16[8,2,17920]{2,1,0:T(2,128)(2,1)} reshape(bf16[2560,2,4,14]{3,2,1,0:T(4,128)(2,1)} %bitcast.53) | data formatting | bytes 1146880
  240.4 20.5 %all-to-all-start = ((bf16[8,2,17920]{2,1,0:T(2,128)(2,1)}), bf16[8,2,17920]{2,1,0:T(2,128)(2,1)S(1)}, u32[]{:S(2)}, u32[]{:S(2)}) async-start(bf16[8,2,17920]{2,1,0:T(2,128)(2,1)} %reshape.77), calls=%async_computation | async-start | bytes 1146880 | tf_op jit(solution)/shard_map/all_to_all | solution.py:113
  261.5 7.9 %all-to-all-done = bf16[8,2,17920]{2,1,0:T(2,128)(2,1)S(1)} async-done(((bf16[8,2,17920]{2,1,0:T(2,128)(2,1)}), bf16[8,2,17920]{2,1,0:T(2,128)(2,1)S(1)}, u32[]{:S(2)}, u32[]{:S(2)}) %all-to-all-start) | async-done | bytes 573472 | tf_op jit(solution)/shard_map/all_to_all | solution.py:113
  269.4 12.7 %reshape.78 = bf16[2560,2,4,14]{3,2,1,0:T(4,128)(2,1)} reshape(bf16[8,2,17920]{2,1,0:T(2,128)(2,1)S(1)} %all-to-all-done) | data formatting | bytes 1146880
  282.1 6.8 %copy.90 = bf16[2,4,14,2560]{3,1,2,0:T(4,128)(2,1)S(1)} copy(bf16[2,4,14,2560]{2,1,0,3:T(4,128)(2,1)} %bitcast.54) | data formatting | bytes 1146880 | tf_op jit(solution)/shard_map/all_to_all | solution.py:113
  288.9 0.5 reshape.61
  289.4 1.1 copy.91
  290.5 0.9 fusion.29
  291.4 129.7 %all-gather.8.cloned.1.call-done = bf16[3,3,320,2560]{3,1,0,2:T(4,128)(2,1)} async-done(((bf16[3,3,20,2560]{3,1,0,2:T(4,128)(2,1)}), bf16[3,3,320,2560]{3,1,0,2:T(4,128)(2,1)}) %all-gather.8.cloned.1.call-update) | async-done | bytes 14745616 | tf_op jit(solution)/shard_map/all_gather | solution.py:129
  421.1 29.9 %conditional.5 = (bf16[2,32,14,2560]{3,1,2,0:T(8,128)(2,1)}) conditional(s32[]{:T(128)} %convert_element_type.59, () %tuple.29, (bf16[2,32,14,320]{3,0,2,1:T(2,128)(2,1)S(1)}, bf16[3,3,320,2560]{3,1,0,2:T(4,128)(2,1)}) %tuple.30), branch_computations={%region_5.6_spmd, %region_6.7_spmd} | conditional | flops 14791475200 | bytes 47022280 | solution.py:125
  422.6 23.2 %fusion.13 = bf16[32,16,2,2560]{3,1,2,0:T(8,128)(2,1)S(1)} fusion(bf16[3,3,320,2560]{3,1,0,2:T(4,128)(2,1)} %get-tuple-element.59, pred[16,2]{0,1:T(4,128)(4,1)S(1)} %copy-done.7, bf16[32,2,7,2,320]{4,2,1,3,0:T(8,128)(2,1)S(1)} %slice.14, bf16[32,2,8,2,320]{4,2,1,3,0:T(8,128)(2,1)S(1)} %copy.82), kind=kOutput, calls=%fused_computation.18 | convolution fusion | flops 14791475200 | bytes 21217312 | tf_op jit(solution)/shard_map/cond/branch_1_fun/conv_general_dilated | solution.py:33
  445.7 2.9 copy.83
  448.6 2.4 slice_bitcast_fusion.1
  451.1 0.6 copy-done.5
  451.7 0.6 dynamic-slice
  453.0 76.3 %all-reduce.3.cloned.1.call-done = bf16[2,32,14,2560]{3,1,2,0:T(8,128)(2,1)} async-done(((bf16[2,32,14,2560]{3,1,2,0:T(8,128)(2,1)}), bf16[2,32,14,2560]{3,1,2,0:T(8,128)(2,1)}) %all-reduce.3.cloned.1.call-update) | async-done | bytes 4587536
  529.3 2.7 fusion.34
  (38 shorter events, 3.0 us)
Async XLA Ops:
  6.5 112.7 %all-gather.4.cloned.1.call-start = ((), (), s32[]{:S(2)}) async-start(), calls=%async_computation.1 | async-start | bytes 7833600 | tf_op jit(solution)/shard_map/all_gather | solution.py:90
  7.3 179.8 %all-gather.6.cloned.1.call-start = ((), (), s32[]{:S(2)}) async-start(), calls=%async_computation.2 | async-start | bytes 3481600 | tf_op jit(solution)/shard_map/all_gather | solution.py:109
  8.0 3.1 copy-start
  8.0 3.1 copy-start.3
  8.0 3.1 copy-start.4
  8.0 413.1 %all-gather.8.cloned.1.call-start = ((), (), s32[]{:S(2)}) async-start(), calls=%async_computation.3 | async-start | bytes 20889600 | tf_op jit(solution)/shard_map/all_gather | solution.py:129
  11.5 4.5 collective-permute-start
  12.8 4.2 collective-permute-start.1
  187.2 20.5 %collective-permute-start.2 = (bf16[2,4,14,2560]{3,1,2,0:T(4,128)(2,1)S(1)}, bf16[2,4,14,2560]{3,1,2,0:T(4,128)(2,1)S(1)}, u32[]{:S(2)}, u32[]{:S(2)}) collective-permute-start(bf16[2,4,14,2560]{3,1,2,0:T(4,128)(2,1)S(1)} %get-tuple-element.60), channel_id=1, source_target_pairs={{0,128},{1,129},{2,130},{3,131},{4,132},{5,133},{6,134},{7,135},{8... | collective-permute-start | bytes 1720328 | tf_op jit(solution)/shard_map/ppermute | solution.py:29
  230.2 30.8 %copy-start.1 = (f32[2560]{0:T(1024)S(1)}, f32[2560]{0:T(1024)}, u32[]{:S(2)}) copy-start(f32[2560]{0:T(1024)} %param.19) | copy-start | bytes 30724
  230.2 30.9 %copy-start.2 = (f32[2560]{0:T(1024)S(1)}, f32[2560]{0:T(1024)}, u32[]{:S(2)}) copy-start(f32[2560]{0:T(1024)} %param.20) | copy-start | bytes 30724
  240.4 28.9 %all-to-all-start = ((bf16[8,2,17920]{2,1,0:T(2,128)(2,1)}), bf16[8,2,17920]{2,1,0:T(2,128)(2,1)S(1)}, u32[]{:S(2)}, u32[]{:S(2)}) async-start(bf16[8,2,17920]{2,1,0:T(2,128)(2,1)} %reshape.77), calls=%async_computation | async-start | bytes 1146880 | tf_op jit(solution)/shard_map/all_to_all | solution.py:113
  261.0 268.3 %all-reduce.3.cloned.1.call-start = ((), (), s32[]{:S(2)}) async-start(), calls=%async_computation.4 | async-start | bytes 9175040
  421.9 0.7 copy-start.7
  451.0 0.7 copy-start.5
Sparse Core Ops, SparseCore 0:
  9.8 109.3 all-gather.3
  121.7 65.2 all-gather.5
  189.6 231.5 all-gather.7
  451.2 78.0 all-reduce.2
where the time goes:
time: 540 us; the launch traced here: 538 us
  waiting for transfers between devices  403 us (75%)
  local copies, waits for them, and re-layouts  66.4 us (12%)
  starting transfers between devices  26.6 us (5%)
  matrix products  23.2 us (4%)
  between operations  14 us (3%)
    all_gather x1, waiting for transfers between devices, body(): lax.all_gather(second_kernel, 'img', axis=2, tiled=True)  130 us
    all_gather x1, waiting for transfers between devices, body(): piece = lax.all_gather(first_kernel, 'img', axis=2, tiled=True)  102 us
    unnamed x5, waiting for transfers between devices  77.7 us
    all_gather x1, waiting for transfers between devices, body(): lax.all_gather(projection, 'img', axis=0, tiled=True)  66 us
    unnamed x16, local copies, waits for them, and re-layouts  27.1 us
    conv_general_dilated x1, matrix products, convolve(): lax.conv_general_dilated(inputs, kernel, (1, 1), padding, dimension_numbe...  23.2 us
    all_to_all x1, starting transfers between devices, body(): lax.all_to_all(sorted_layout, 'ch', split_axis=3, concat_axis=1, tiled=True)  20.5 us
    ppermute x1, waiting for transfers between devices, from_behind(): return lax.ppermute(array, axis, pairs)  19.1 us
  transfers between devices with their start and end apart: 8, of which 7 were waited for; matrix products, arithmetic and copies ran while one was open for 11% of the time, Pallas kernels for 0%

commit v1 on v0

v1 whole, which is shorter than its diff:
```python
import jax
import jax.numpy as jnp
from jax import lax
from jax.experimental import pallas as pl
from jax.experimental.pallas import tpu as pltpu
from jax.sharding import PartitionSpec as P

MESH = pl.DeviceIdType.MESH
F32 = jnp.float32
BF16 = jnp.bfloat16
D = 640
SLAB = 160


def lanes(i):
    return pl.ds(pl.multiple_of(i * D, 128), D)


def rows(i, n):
    return pl.ds(pl.multiple_of(i * n, 16), n)


def dot(a, b):
    return jnp.dot(a, b, preferred_element_type=F32)


def kernel(
    pix, g1, s1, k1, pr, g2, s2, k2,
    out,
    pxp, hal_t, hal_b, wp, wy, pland, wall, pn, k1x, nb, nsel, bq, acc1, part, prx, rtmp,
    pb, plin, pjb, abuf, acc2, cp, cin, fb,
    s_px, r_px, s_ht, r_ht, s_hb, r_hb, s_k1, r_k1, s_kx, r_kx, s_pr, r_pr, s_wy, r_wy,
    s_h1, r_h1, s_h2, r_h2, s_h3, r_h3, s_dd, r_dd, s_pa, r_pa, s_pl, r_pl,
    s_pj, r_pj, s_c, r_c, s_f, r_f,
):
    s = lax.axis_index("section")
    img = lax.axis_index("img")
    ch = lax.axis_index("ch")
    x, zh = lax.div(img, 4), lax.rem(img, 4)
    y, c = lax.div(ch, 2), lax.rem(ch, 2)
    other = 1 - c
    way = 2 * s - 1

    def dev(s_, x_, zh_, y_, c_):
        return (s_, lax.rem(x_ + 8, 4) * 4 + lax.rem(zh_ + 8, 4), lax.rem(y_ + 8, 4) * 2 + c_)

    def remote(src, dst, ss, rs, to):
        return pltpu.make_async_remote_copy(
            src_ref=src, dst_ref=dst, send_sem=ss, recv_sem=rs, device_id=to, device_id_type=MESH
        )

    partner = dev(s, x, zh, y, other)
    pair = dev(1 - s, x, zh, y, c)
    outward = dev(1 - s, x, zh + way, y, c)

    def arrived(dst, rs):
        remote(dst, dst, rs, rs, partner).wait_recv()

    barrier = pltpu.get_barrier_semaphore()
    met = []
    for dx in range(4):
        for dy in range(4):
            for dc in range(2):
                if dx or dy or dc:
                    met.append(dev(s, x + dx, zh, y + dy, c if dc == 0 else other))
    for dx in range(4):
        for dc in range(2):
            met.append(dev(1 - s, x + dx, zh, y, c if dc == 0 else other))
    met.append(outward)
    met.append(dev(1 - s, x, zh + 2, y, c))
    for to in met:
        pl.semaphore_signal(barrier, inc=1, device_id=to, device_id_type=MESH)
    pl.semaphore_wait(barrier, len(met))

    px_copy = remote(pix, pxp, s_px, r_px, partner)
    px_copy.start()
    down = [
        remote(pix.at[:, pl.ds(7, 1)], hal_t, s_ht.at[k], r_ht, dev(s, x, zh, y + 1, k))
        for k in range(2)
    ]
    up = [
        remote(pix.at[:, pl.ds(0, 1)], hal_b, s_hb.at[k], r_hb, dev(s, x, zh, y - 1, k))
        for k in range(2)
    ]
    sends_down = jnp.logical_and(c == 1, y < 3)
    sends_up = jnp.logical_and(c == 0, y > 0)

    @pl.when(sends_down)
    def _():
        for cpy in down:
            cpy.start()

    @pl.when(sends_up)
    def _():
        for cpy in up:
            cpy.start()

    zq_off = (1 - s) * 3 * c + s * (1 + c)
    zq = lax.rem(zh + zq_off, 4)
    k1_sends = jnp.logical_not(jnp.logical_and(s == 1, c == 0))
    k1_gets = jnp.logical_not(jnp.logical_and(s == 0, c == 0))
    k1_to = dev(1 - s, x, zh + s - (1 - s) * (1 + c), y, c)
    k1_copies = [
        remote(k1.at[pl.ds(3 * q, 3)], k1x.at[x, pl.ds(3 * q, 3)], s_k1.at[q], r_k1.at[q], k1_to)
        for q in range(3)
    ]

    @pl.when(k1_sends)
    def _():
        for cpy in k1_copies:
            cpy.start()

    @pl.when(jnp.logical_not(k1_gets))
    def _():
        k1x[x] = k1[...]

    pr_copies = []
    for dx in range(1, 4):
        to = lax.rem(x + dx, 4)
        cpy = remote(
            pr.at[:, lanes(to)], pland.at[x], s_pr.at[dx - 1], r_pr.at[dx - 1], dev(s, to, zh, y, c)
        )
        cpy.start()
        pr_copies.append(cpy)
    pland[x] = pr[:, lanes(x)]

    for half, first, count in ((0, 0, 5), (1, 5, 4)):
        for t in range(count):
            wp[half, pl.ds(20 * t, 20), :] = k2[first + t]
        wp[half, pl.ds(20 * count, 112 - 20 * count), :] = jnp.zeros((112 - 20 * count, 4 * D), BF16)
    wy_copies = []
    for dy in range(4):
        for dc in range(2):
            if dy == 0 and dc == 0:
                continue
            ty = lax.rem(y + dy, 4)
            tc = c if dc == 0 else other
            k = dy * 2 + dc
            cpy = remote(
                wp.at[tc, :, lanes(ty)], wy.at[ch], s_wy.at[k], r_wy.at[k], dev(s, x, zh, ty, tc)
            )
            cpy.start()
            wy_copies.append(cpy)
    wy[ch] = wp[c, :, lanes(y)]

    nsel[...] = jnp.zeros_like(nsel)
    for k in range(3):
        for e in range(2):
            abuf[k, e, pl.ds(0, 16), :] = jnp.zeros((16, D), BF16)
            abuf[k, e, pl.ds(528, 16), :] = jnp.zeros((16, D), BF16)

    def norm(cells):
        n = jnp.maximum(cells.astype(F32) * g1[...] + s1[...], 0.0)
        return jnp.concatenate([n, jnp.zeros((4, D), F32)], axis=0).astype(BF16)

    def norm_rows(ref, base):
        def step(i, carry):
            e, r = lax.div(i, 8), lax.rem(i, 8)
            nb[e, base + r] = norm(ref[e, r])
            return carry

        lax.fori_loop(0, 16, step, 0)

    norm_rows(pix, 1 + 8 * c)

    for i in range(4):
        both = pix[s, 2 * i].astype(F32) + pix[s, 2 * i + 1].astype(F32)
        both = jnp.concatenate([both, jnp.zeros((4, D), F32)], axis=0)
        for b in range(5):
            rtmp[i, b] = both[:, 128 * b : 128 * b + 128]

    kx_copies = []

    def k1_forward(q):
        @pl.when(k1_gets)
        def _():
            arrived(k1x.at[x, pl.ds(3 * q, 3)], r_k1.at[q])

        for dx in range(1, 4):
            block = k1x.at[x, pl.ds(3 * q, 3)]
            cpy = remote(
                block, block, s_kx.at[dx - 1, q], r_kx.at[dx - 1, q], dev(s, x + dx, zh, y, c)
            )
            cpy.start()
            kx_copies.append(cpy)

    for q in range(3):
        k1_forward(q)

    for dy in range(4):
        for dc in range(2):
            if dy or dc:
                sy = lax.rem(y - dy + 4, 4)
                sc = c if dc == 0 else other
                arrived(wy.at[sy * 2 + sc], r_wy.at[dy * 2 + dc])
    for dx in range(1, 4):
        arrived(pland.at[lax.rem(x - dx + 4, 4)], r_pr.at[dx - 1])

    def packed(t):
        return jnp.concatenate([wy[k, pl.ds(20 * t, 20), :] for k in range(8)], axis=0)

    def at(core, j, z_):
        return wall.at[5 * core + j, rows(z_, SLAB)]

    @pl.when(c == 0)
    def _():
        for j in range(5):
            wall[j, rows(zh, SLAB), :] = packed(j)

    @pl.when(c == 1)
    def _():
        wall[5, rows(zh, SLAB), :] = jnp.concatenate([pland[k] for k in range(4)], axis=0)
        for j in range(1, 5):
            wall[5 + j, rows(zh, SLAB), :] = packed(j - 1)

    z1 = lax.rem(zh + way + 4, 4)
    z2 = lax.rem(zh - way + 4, 4)
    z3 = lax.rem(zh + 2, 4)
    zs = (zh, z1, z2, z3)
    chain = []

    def share(q, j):
        cpy = remote(at(c, j, zs[q]), at(c, j, zs[q]), s_dd.at[q, j], r_dd.at[q, j], partner)
        cpy.start()
        chain.append(cpy)

    def pass_on(q, j, ss, rs, to):
        cpy = remote(at(c, j, zs[q]), at(c, j, zs[q]), ss.at[j], rs.at[j], to)
        cpy.start()
        chain.append(cpy)

    for j in range(5):
        pass_on(0, j, s_h1, r_h1, outward)
    for j in range(5):
        share(0, j)

    def hop1(j):
        arrived(at(c, j, z1), r_h1.at[j])
        pass_on(1, j, s_h2, r_h2, pair)
        share(1, j)

    def hop2(j):
        arrived(at(c, j, z2), r_h2.at[j])
        pass_on(2, j, s_h3, r_h3, outward)
        share(2, j)

    def hop3(j):
        arrived(at(c, j, z3), r_h3.at[j])
        share(3, j)

    arrived(pxp, r_px)
    norm_rows(pxp, 1 + 8 * other)

    @pl.when(y > 0)
    def _():
        arrived(hal_t, r_ht)
        for e in range(2):
            nb[e, 0] = norm(hal_t[e, 0])

    @pl.when(y == 0)
    def _():
        nb[:, 0] = jnp.zeros((2, 32, D), BF16)

    @pl.when(y < 3)
    def _():
        arrived(hal_b, r_hb)
        for e in range(2):
            nb[e, 17] = norm(hal_b[e, 0])

    @pl.when(y == 3)
    def _():
        nb[:, 17] = jnp.zeros((2, 32, D), BF16)

    col = lax.broadcasted_iota(jnp.int32, (D, 256), 1)
    row = lax.broadcasted_iota(jnp.int32, (D, 256), 0)
    want = jnp.where(col < 160, col + lax.div(col, 40) * 120 + zq * 40, -1)
    select = jnp.where(row == want, 1.0, 0.0).astype(BF16)

    def select_rows(i, carry):
        e, b = lax.div(i, 3), lax.rem(i, 3)
        got = dot(nb[e, pl.ds(6 * b, 6)].reshape(192, D), select)
        for r in range(6):
            for h in range(2):
                nsel[h, e, 6 * b + r, pl.ds(8, 32), :] = got[32 * r : 32 * r + 32, 128 * h : 128 * h + 128]
        return carry

    lax.fori_loop(0, 6, select_rows, 0)

    def box(i, carry):
        e, r = lax.div(i, 9), lax.rem(i, 9)
        for par in range(2):
            for h in range(2):
                v = [
                    nsel[h, e, 2 * r + par, pl.ds(7 + d, 16, stride=2), :]
                    + nsel[h, e, 2 * r + par + 1, pl.ds(7 + d, 16, stride=2), :]
                    for d in range(4)
                ]
                for dx in range(3):
                    both = ((v[dx] + v[dx + 1]) * 0.25).astype(BF16)
                    bq[dx, par, e, r, :, pl.ds(128 * h, 128)] = both
        return carry

    lax.fori_loop(0, 18, box, 0)

    hop1(0)
    hop1(1)

    for dx in range(1, 4):
        for q in range(3):
            arrived(k1x.at[lax.rem(x - dx + 4, 4), pl.ds(3 * q, 3)], r_kx.at[dx - 1, q])
    for t in range(9):
        dy, dx = t // 3, t % 3
        w = jnp.concatenate([k1x[k, t] for k in range(4)], axis=0)
        a = bq[dx, dy % 2, :, pl.ds(dy // 2, 8), :, :].reshape(256, 256)[:, :160]
        got = dot(a, w)
        if t == 0:
            acc1[...] = got
        else:
            acc1[...] += got
    part[...] = acc1[...].astype(BF16)
    pa_copies = []
    for k in range(1, 4):
        ts = s if k < 2 else 1 - s
        tc = c if k % 2 == 0 else other
        cpy = remote(
            part.at[rows(ts * 2 + tc, 64)], prx.at[k - 1], s_pa.at[k - 1], r_pa.at[k - 1],
            dev(ts, x, zh, y, tc),
        )
        cpy.start()
        pa_copies.append(cpy)
    hop1(2)
    for k in range(3):
        arrived(prx.at[k], r_pa.at[k])
    total = acc1[rows(s * 2 + c, 64), :]
    for k in range(3):
        total += prx[k].astype(F32)
    rest = jnp.concatenate(
        [
            jnp.concatenate(
                [
                    rtmp[i, b, pl.ds(0, 16, stride=2), :] + rtmp[i, b, pl.ds(1, 16, stride=2), :]
                    for b in range(5)
                ],
                axis=1,
            )
            for i in range(4)
        ],
        axis=0,
    )
    pb[...] = (total + rest * 0.25).astype(BF16)

    core = lax.div(x, 2)
    slot = lax.rem(x, 2)
    pl_copies = []
    for dx in range(4):
        for dy in range(4):
            k = dx * 4 + dy
            cpy = remote(
                pb, plin.at[slot, rows(ch, 64)], s_pl.at[k], r_pl.at[slot * 8 + ch],
                dev(s, x + dx, zh, y + dy, core),
            )
            pl_copies.append(cpy)
            if k:
                cpy.start()

    @pl.when(core != c)
    def _():
        pl_copies[0].start()

    @pl.when(core == c)
    def _():
        plin[slot, rows(ch, 64), :] = pb[...]

    for j in range(3, 5):
        hop1(j)
    for j in range(5):
        hop2(j)
    hop3(0)

    for e in range(2):
        for k in range(8):
            own = jnp.logical_and(2 * c + e == x, ch == k)

            @pl.when(jnp.logical_not(own))
            def _(e=e, k=k):
                arrived(plin.at[e, pl.ds(64 * k, 64)], r_pl.at[e * 8 + k])

    @pl.when(c == 0)
    def _():
        for q in range(4):
            arrived(at(1, 0, zs[q]), r_dd.at[q, 0])

    pn[...] = jnp.concatenate(
        [wall[5, pl.ds(zb * SLAB + xb * 40, 40), :] for xb in range(4) for zb in range(4)], axis=0
    )
    gain, shift = g2[:, lanes(x)], s2[:, lanes(x)]
    inside = lax.rem(lax.broadcasted_iota(jnp.int32, (128, 1), 0), 16) < 14

    def project(i, carry):
        e, m = lax.div(i, 4), lax.rem(i, 4)
        p = dot(plin[e, rows(m, 128), :], pn[...]).astype(BF16)
        pjb[e, rows(m, 128), :] = p
        v = jnp.maximum(p.astype(F32) * gain + shift, 0.0)
        v = jnp.where(inside, v, 0.0)
        place = pl.ds(pl.multiple_of(128 * m + 16, 16), 128)
        abuf[0, e, place, :] = pltpu.roll(v, 1, 0).astype(BF16)
        abuf[1, e, place, :] = v.astype(BF16)
        abuf[2, e, place, :] = pltpu.roll(v, 127, 0).astype(BF16)
        return carry

    lax.fori_loop(0, 8, project, 0)

    pj_copies = []
    for e in range(2):
        for tc in range(2):
            own = jnp.logical_and(jnp.logical_and(s == 0, 2 * c + e == x), tc == c)
            src = pjb.at[e, rows(2 * y + tc, 64)]
            cpy = remote(
                src, out.at[s, :, lanes(x)], s_pj.at[2 * e + tc], r_pj.at[4 * s + x],
                dev(0, 2 * c + e, zh, y, tc),
            )
            pj_copies.append((own, cpy))

            @pl.when(jnp.logical_not(own))
            def _(cpy=cpy):
                cpy.start()

            @pl.when(own)
            def _(src=src):
                out[0, :, lanes(x)] = src[...]

    for j in range(1, 5):
        hop3(j)
    for q in range(4):
        for j in range(5):
            if j == 0:

                @pl.when(c == 1)
                def _(q=q):
                    arrived(at(0, 0, zs[q]), r_dd.at[q, 0])

            else:
                arrived(at(other, j, zs[q]), r_dd.at[q, j])

    adds = x == y

    def c_copy(e, k):
        return remote(
            cp.at[e, rows(k, 64)], cin.at[x * 4 + y], s_c.at[e * 8 + k], r_c.at[x * 4 + y],
            dev(s, 2 * c + e, zh, lax.div(k, 2), lax.rem(k, 2)),
        )

    def c_own(e, k):
        return jnp.logical_and(2 * c + e == x, k == ch)

    def second(i, carry):
        e, m = lax.div(i, 2), lax.rem(i, 2)
        for t in range(9):
            dy, dx = t // 3, t % 3
            a = abuf[dx, e, pl.ds(pl.multiple_of(256 * m + 16 * dy, 16), 256), :]
            got = dot(a, wall[t if t < 5 else t + 1])
            if t == 0:
                acc2[...] = got
            else:
                acc2[...] += got
        proj = pjb[e, rows(m, 256), :].astype(F32)
        cp[e, rows(m, 256), :] = (acc2[...] + jnp.where(adds, proj, 0.0)).astype(BF16)
        for q in range(4):
            k = 4 * m + q
            own = c_own(e, k)

            @pl.when(jnp.logical_not(own))
            def _(k=k):
                c_copy(e, k).start()

            @pl.when(own)
            def _(k=k):
                cin[x * 4 + y] = cp[e, rows(k, 64), :]

        return carry

    lax.fori_loop(0, 4, second, 0)

    f_copies = []
    for yb in range(4):
        total = jnp.zeros((64, D), F32)
        for xb in range(4):
            own = jnp.logical_and(jnp.logical_and(core == c, xb == x), yb == y)

            @pl.when(jnp.logical_not(own))
            def _(xb=xb, yb=yb):
                arrived(cin.at[xb * 4 + yb], r_c.at[xb * 4 + yb])

            total += cin[xb * 4 + yb].astype(F32)
        columns = pl.ds(yb * D, D)
        fb[:, columns] = total.astype(BF16)
        cpy = remote(fb.at[:, columns], out.at[0, :, columns], s_f.at[yb], r_f.at[yb], pair)
        f_copies.append(cpy)

        @pl.when(s == 0)
        def _(cpy=cpy):
            cpy.start()

        @pl.when(s == 1)
        def _(columns=columns):
            out[1, :, columns] = fb[:, columns]

    @pl.when(s == 0)
    def _():
        for sb in range(2):
            for xb in range(4):
                own = jnp.logical_and(jnp.logical_and(sb == 0, xb == x), core == c)

                @pl.when(jnp.logical_not(own))
                def _(sb=sb, xb=xb):
                    arrived(out.at[sb, :, pl.ds(xb * D, D)], r_pj.at[4 * sb + xb])

        for cpy in f_copies:
            cpy.wait_send()

    @pl.when(s == 1)
    def _():
        for yb in range(4):
            arrived(out.at[0, :, pl.ds(yb * D, D)], r_f.at[yb])

    for own, cpy in pj_copies:

        @pl.when(jnp.logical_not(own))
        def _(cpy=cpy):
            cpy.wait_send()

    for e in range(2):
        for k in range(8):

            @pl.when(jnp.logical_not(c_own(e, k)))
            def _(e=e, k=k):
                c_copy(e, k).wait_send()

    px_copy.wait_send()

    @pl.when(sends_down)
    def _():
        for cpy in down:
            cpy.wait_send()

    @pl.when(sends_up)
    def _():
        for cpy in up:
            cpy.wait_send()

    @pl.when(k1_sends)
    def _():
        for cpy in k1_copies:
            cpy.wait_send()

    @pl.when(core != c)
    def _():
        pl_copies[0].wait_send()

    for cpy in pr_copies + wy_copies + kx_copies + chain + pa_copies + pl_copies[1:]:
        cpy.wait_send()


def body(
    pixels,
    first_gain,
    first_shift,
    first_kernel,
    projection,
    second_gain,
    second_shift,
    second_kernel,
):
    dma = pltpu.SemaphoreType.DMA

    def vmem(*shape, dtype=BF16):
        return pltpu.VMEM(shape, dtype)

    counts = [
        (), (), (2,), (), (2,), (), (3,), (3,), (3, 3), (3, 3), (3,), (3,), (8,), (8,),
        (5,), (5,), (5,), (5,), (5,), (5,), (4, 5), (4, 5), (3,), (3,), (16,), (16,),
        (4,), (8,), (16,), (16,), (4,), (4,),
    ]
    result = pl.pallas_call(
        kernel,
        name="window",
        out_shape=jax.ShapeDtypeStruct((2, 64, 4 * D), BF16),
        in_specs=[pl.BlockSpec(memory_space=pltpu.VMEM)] * 8,
        out_specs=pl.BlockSpec(memory_space=pltpu.VMEM),
        scratch_shapes=[
            vmem(2, 8, 28, D),
            vmem(2, 1, 28, D),
            vmem(2, 1, 28, D),
            vmem(2, 112, 4 * D),
            vmem(8, 112, D),
            vmem(4, 40, D),
            vmem(10, D, D),
            vmem(D, D),
            vmem(4, 9, 40, D),
            vmem(2, 18, 32, D),
            vmem(2, 2, 19, 48, 128, dtype=F32),
            vmem(3, 2, 2, 9, 16, 256),
            vmem(256, D, dtype=F32),
            vmem(256, D),
            vmem(3, 64, D),
            vmem(4, 5, 32, 128, dtype=F32),
            vmem(64, D),
            vmem(2, 512, D),
            vmem(2, 512, D),
            vmem(3, 2, 544, D),
            vmem(256, D, dtype=F32),
            vmem(2, 512, D),
            vmem(16, 64, D),
            vmem(64, 4 * D),
        ]
        + [dma(n) for n in counts],
        compiler_params=pltpu.CompilerParams(
            collective_id=0, has_side_effects=True, vmem_limit_bytes=56 * 2**20
        ),
        cost_estimate=pl.CostEstimate(flops=8 * 10**9, bytes_accessed=10**7, transcendentals=0),
    )(
        pixels,
        first_gain[None],
        first_shift[None],
        first_kernel.reshape(9, 40, D),
        projection,
        second_gain[None],
        second_shift[None],
        second_kernel.reshape(9, 20, 4 * D),
    )
    return result.reshape(2, 4, 16, 4 * D)[None, :, :, :14]


def solution(mesh):
    placed = (
        P("img", "ch", None, None),
        P(),
        P(),
        P(None, None, "img", None),
        P("img", None),
        P(),
        P(),
        P(None, None, ("img", "ch"), None),
    )
    return jax.shard_map(
        body,
        mesh=mesh,
        in_specs=placed,
        out_specs=P("section", "img", "ch", None, None),
        check_vma=False,
    )
```

time: 540 us -> 124 us (0.23)
  waiting for transfers between devices: 403 us -> 0 us
  Pallas kernels: 0 us -> 113 us
  local copies, waits for them, and re-layouts: 66.4 us -> 9.48 us
  starting transfers between devices: 26.6 us -> 0 us
  matrix products: 23.2 us -> 0 us
  between operations: 14 us -> 0.01 us
    all_gather x3 -> x0, waiting for transfers between devices: 297 us -> none  [the longest x1 130 us: body(): lax.all_gather(second_kernel, 'img', axis=2, tiled=True)]
    pallas_call x0 -> x1, Pallas kernels: none -> 113 us  [body(): pl.pallas_call(kernel, name='window', out_shape=jax.ShapeDtypeStruct((2,...]
    unnamed x5 -> x0, waiting for transfers between devices: 77.7 us -> none
    conv_general_dilated x1 -> x0, matrix products: 23.2 us -> none  [convolve(): lax.conv_general_dilated(inputs, kernel, (1, 1), padding, dimension_numbe...]
    unnamed x16 -> x2, local copies, waits for them, and re-layouts: 27.1 us -> 4.31 us
    reshape x5 -> x0, local copies, waits for them, and re-layouts: 22.8 us -> none  [the longest x1 12.8 us: arrange_groups(): return swapped.reshape(lead + (groups * shards * per_block,))]
    all_to_all x1 -> x0, starting transfers between devices: 20.5 us -> none  [body(): lax.all_to_all(sorted_layout, 'ch', split_axis=3, concat_axis=1, tiled=True)]
    ppermute x3 -> x0, waiting for transfers between devices: 20 us -> none  [the longest x1 19.1 us: from_behind(): return lax.ppermute(array, axis, pairs)]
  transfers between devices with their start and end apart: 8 -> 0, of which waited for: 7 -> 0; matrix products, arithmetic and copies ran while one was open for 11% -> 0% of each run, Pallas kernels for 0% -> 0%
where the time goes in v1:
time: 124 us; the launch traced here: 123 us
  Pallas kernels  113 us (91%)
  local copies, waits for them, and re-layouts  9.48 us (8%)
    pallas_call x1, Pallas kernels, body(): pl.pallas_call(kernel, name='window', out_shape=jax.ShapeDtypeStruct((2,...  113 us
    unnamed x2, local copies, waits for them, and re-layouts  4.31 us

profile of v1, /device:TPU:59, one launch (start us, length us, event | category | flops | bytes accessed | tf_op | source)
XLA Modules:
  0.0 122.9 jit_solution(9116635167937962705)
XLA Ops:
  0.0 1.3 %broadcast_in_dim.15.g1 = f32[1,640]{1,0:T(1,128)} reshape(f32[640]{0:T(1024)} %param.9) | data formatting | bytes 5120 | tf_op jit(solution)/shard_map/broadcast_in_dim | solution.py:623
  1.3 1.3 %broadcast_in_dim.16.s1 = f32[1,640]{1,0:T(1,128)} reshape(f32[640]{0:T(1024)} %param.10) | data formatting | bytes 5120 | tf_op jit(solution)/shard_map/broadcast_in_dim | solution.py:624
  2.5 1.3 %broadcast_in_dim.17.g2 = f32[1,2560]{1,0:T(1,128)} reshape(f32[2560]{0:T(1024)} %param.13) | data formatting | bytes 20480 | tf_op jit(solution)/shard_map/broadcast_in_dim | solution.py:627
  3.9 1.3 %broadcast_in_dim.18.s2 = f32[1,2560]{1,0:T(1,128)} reshape(f32[2560]{0:T(1024)} %param.14) | data formatting | bytes 20480 | tf_op jit(solution)/shard_map/broadcast_in_dim | solution.py:628
  5.2 2.0 %copy.9.pix = bf16[2,8,28,640]{3,2,1,0:T(8,128)(2,1)} copy(bf16[2,8,28,640]{3,1,2,0:T(8,128)(2,1)} %param.8) | data formatting | bytes 1146880 | tf_op args[0]
  7.1 113.5 %window.1 = bf16[2,64,2560]{2,1,0:T(8,128)(2,1)} custom-call(bf16[2,8,28,640]{3,2,1,0:T(8,128)(2,1)} %copy.9.pix, f32[1,640]{1,0:T(1,128)} %broadcast_in_dim.15.g1, f32[1,640]{1,0:T(1,128)} %broadcast_in_dim.16.s1, bf16[9,40,640]{2,1,0:T(8,128)(2,1)} %bitcast.9, bf16[40,2560]{1,0:T(8,128)(2,1)} %pr.1, f32[1,2560]{1,0:T(1,128)} %broadcast_in_dim.17.g2, ...), custom_call_target="tpu_custom_call" | custom-call | flops 8000000000 | bytes 10000000 | tf_op jit(solution)/shard_map/window/pallas_call | solution.py:584
  120.6 2.3 %copy.13 = bf16[2,4,14,2560]{3,1,2,0:T(4,128)(2,1)} copy(bf16[2,4,14,2560]{3,2,1,0:T(8,128)(2,1)} %bitcast.7) | data formatting | bytes 1146880

commit v2 on v1

--- a/solution.py
+++ b/solution.py
@@ -28,9 +28,9 @@
     pix, g1, s1, k1, pr, g2, s2, k2,
     out,
     pxp, hal_t, hal_b, wp, wy, pland, wall, pn, k1x, nb, nsel, bq, acc1, part, prx, rtmp,
-    pb, plin, pjb, abuf, acc2, cp, cin, fb,
+    pb, plin, pjb, abuf, acc2, cp, cin, fb, g2w, s2w,
     s_px, r_px, s_ht, r_ht, s_hb, r_hb, s_k1, r_k1, s_kx, r_kx, s_pr, r_pr, s_wy, r_wy,
-    s_h1, r_h1, s_h2, r_h2, s_h3, r_h3, s_dd, r_dd, s_pa, r_pa, s_pl, r_pl,
+    s_h1, r_h1, s_h2, r_h2, s_h3, r_h3, s_h4, r_h4, s_dd, r_dd, s_pa, r_pa, s_pl, r_pl,
     s_pj, r_pj, s_c, r_c, s_f, r_f,
 ):
     s = lax.axis_index("section")
@@ -70,7 +70,14 @@
     met.append(dev(1 - s, x, zh + 2, y, c))
     for to in met:
         pl.semaphore_signal(barrier, inc=1, device_id=to, device_id_type=MESH)
-    pl.semaphore_wait(barrier, len(met))
+    diagonal = jnp.logical_and(c == 1, x == y)
+
+    @pl.when(jnp.logical_and(c == 1, x != y))
+    def _():
+        to = dev(1 - s, y, zh - (1 - s) + 2 * s, y, c)
+        pl.semaphore_signal(barrier, inc=1, device_id=to, device_id_type=MESH)
+
+    pl.semaphore_wait(barrier, len(met) + jnp.where(diagonal, 3, 0))
 
     px_copy = remote(pix, pxp, s_px, r_px, partner)
     px_copy.start()
@@ -97,18 +104,30 @@
 
     zq_off = (1 - s) * 3 * c + s * (1 + c)
     zq = lax.rem(zh + zq_off, 4)
-    k1_sends = jnp.logical_not(jnp.logical_and(s == 1, c == 0))
+    line = jnp.where(c == 0, x, y)
     k1_gets = jnp.logical_not(jnp.logical_and(s == 0, c == 0))
-    k1_to = dev(1 - s, x, zh + s - (1 - s) * (1 + c), y, c)
+    k1_sends = jnp.logical_and(c == 0, s == 0)
     k1_copies = [
-        remote(k1.at[pl.ds(3 * q, 3)], k1x.at[x, pl.ds(3 * q, 3)], s_k1.at[q], r_k1.at[q], k1_to)
-        for q in range(3)
+        [
+            remote(
+                k1.at[pl.ds(3 * q, 3)], k1x.at[line, pl.ds(3 * q, 3)], s_k1.at[dx, q], r_k1.at[q],
+                dev(1 - s, x + dx, zh + s - (1 - s) * (1 + c), y, c),
+            )
+            for q in range(3)
+        ]
+        for dx in range(4)
     ]
 
     @pl.when(k1_sends)
     def _():
-        for cpy in k1_copies:
+        for cpy in k1_copies[0]:
             cpy.start()
+
+    @pl.when(diagonal)
+    def _():
+        for q in range(3):
+            for dx in (2, 1, 3, 0):
+                k1_copies[dx][q].start()
 
     @pl.when(jnp.logical_not(k1_gets))
     def _():
@@ -124,25 +143,34 @@
         pr_copies.append(cpy)
     pland[x] = pr[:, lanes(x)]
 
-    for half, first, count in ((0, 0, 5), (1, 5, 4)):
-        for t in range(count):
-            wp[half, pl.ds(20 * t, 20), :] = k2[first + t]
-        wp[half, pl.ds(20 * count, 112 - 20 * count), :] = jnp.zeros((112 - 20 * count, 4 * D), BF16)
     wy_copies = []
-    for dy in range(4):
-        for dc in range(2):
-            if dy == 0 and dc == 0:
-                continue
-            ty = lax.rem(y + dy, 4)
-            tc = c if dc == 0 else other
-            k = dy * 2 + dc
-            cpy = remote(
-                wp.at[tc, :, lanes(ty)], wy.at[ch], s_wy.at[k], r_wy.at[k], dev(s, x, zh, ty, tc)
-            )
-            cpy.start()
-            wy_copies.append(cpy)
+    for part_at, size, taps in ((0, 48, (0, 1)), (48, 64, (2, 3, 4))):
+        for half, first, count in ((0, 0, 5), (1, 5, 4)):
+            used = 0
+            for a in taps:
+                if a < count:
+                    wp[half, pl.ds(part_at + used, 20), :] = k2[first + a]
+                    used += 20
+            blank = size - used
+            wp[half, pl.ds(part_at + used, blank), :] = jnp.zeros((blank, 4 * D), BF16)
+        for dy in (2, 1, 3, 0):
+            for dc in range(2):
+                if dy == 0 and dc == 0:
+                    continue
+                ty = lax.rem(y + dy, 4)
+                tc = c if dc == 0 else other
+                k = (part_at // 48) * 8 + dy * 2 + dc
+                cpy = remote(
+                    wp.at[tc, pl.ds(part_at, size), lanes(ty)], wy.at[ch, pl.ds(part_at, size)],
+                    s_wy.at[k], r_wy.at[k], dev(s, x, zh, ty, tc),
+                )
+                cpy.start()
+                wy_copies.append(cpy)
     wy[ch] = wp[c, :, lanes(y)]
 
+    g2w[...] = g2[...].reshape(1, 4 * D)
+    s2w[...] = s2[...].reshape(1, 4 * D)
+    gain1, shift1 = g1[...].reshape(1, D), s1[...].reshape(1, D)
     nsel[...] = jnp.zeros_like(nsel)
     for k in range(3):
         for e in range(2):
@@ -150,7 +178,7 @@
             abuf[k, e, pl.ds(528, 16), :] = jnp.zeros((16, D), BF16)
 
     def norm(cells):
-        n = jnp.maximum(cells.astype(F32) * g1[...] + s1[...], 0.0)
+        n = jnp.maximum(cells.astype(F32) * gain1 + shift1, 0.0)
         return jnp.concatenate([n, jnp.zeros((4, D), F32)], axis=0).astype(BF16)
 
     def norm_rows(ref, base):
@@ -172,81 +200,115 @@
     kx_copies = []
 
     def k1_forward(q):
+        block = k1x.at[line, pl.ds(3 * q, 3)]
+
         @pl.when(k1_gets)
         def _():
-            arrived(k1x.at[x, pl.ds(3 * q, 3)], r_k1.at[q])
-
-        for dx in range(1, 4):
-            block = k1x.at[x, pl.ds(3 * q, 3)]
+            arrived(block, r_k1.at[q])
+
+        for d in (2, 1, 3):
             cpy = remote(
-                block, block, s_kx.at[dx - 1, q], r_kx.at[dx - 1, q], dev(s, x + dx, zh, y, c)
+                block, block, s_kx.at[d - 1, q], r_kx.at[d - 1, q],
+                dev(s, x + d * (1 - c), zh, y + d * c, c),
             )
             cpy.start()
             kx_copies.append(cpy)
 
-    for q in range(3):
-        k1_forward(q)
-
-    for dy in range(4):
-        for dc in range(2):
-            if dy or dc:
-                sy = lax.rem(y - dy + 4, 4)
-                sc = c if dc == 0 else other
-                arrived(wy.at[sy * 2 + sc], r_wy.at[dy * 2 + dc])
-    for dx in range(1, 4):
-        arrived(pland.at[lax.rem(x - dx + 4, 4)], r_pr.at[dx - 1])
-
-    def packed(t):
-        return jnp.concatenate([wy[k, pl.ds(20 * t, 20), :] for k in range(8)], axis=0)
+    def wy_wait(part_at, size):
+        for dy in range(4):
+            for dc in range(2):
+                if dy or dc:
+                    sy = lax.rem(y - dy + 4, 4)
+                    sc = c if dc == 0 else other
+                    k = (part_at // 48) * 8 + dy * 2 + dc
+                    arrived(wy.at[sy * 2 + sc, pl.ds(part_at, size)], r_wy.at[k])
+
+    def packed(a):
+        at_row = 20 * a if a < 2 else 48 + 20 * (a - 2)
+        return jnp.concatenate([wy[k, pl.ds(at_row, 20), :] for k in range(8)], axis=0)
 
     def at(core, j, z_):
         return wall.at[5 * core + j, rows(z_, SLAB)]
-
-    @pl.when(c == 0)
-    def _():
-        for j in range(5):
-            wall[j, rows(zh, SLAB), :] = packed(j)
-
-    @pl.when(c == 1)
-    def _():
-        wall[5, rows(zh, SLAB), :] = jnp.concatenate([pland[k] for k in range(4)], axis=0)
-        for j in range(1, 5):
-            wall[5 + j, rows(zh, SLAB), :] = packed(j - 1)
 
     z1 = lax.rem(zh + way + 4, 4)
     z2 = lax.rem(zh - way + 4, 4)
     z3 = lax.rem(zh + 2, 4)
     zs = (zh, z1, z2, z3)
     chain = []
-
-    def share(q, j):
-        cpy = remote(at(c, j, zs[q]), at(c, j, zs[q]), s_dd.at[q, j], r_dd.at[q, j], partner)
+    shares = []
+    side = lax.rem(s + c, 2)
+
+    def share(q, j, n):
+        k = len(shares)
+        shares.append((q, j, n))
+        block = wall.at[pl.ds(5 * c + j, n), rows(zs[q], SLAB)]
+        cpy = remote(block, block, s_dd.at[k], r_dd.at[k], partner)
         cpy.start()
         chain.append(cpy)
 
-    def pass_on(q, j, ss, rs, to):
-        cpy = remote(at(c, j, zs[q]), at(c, j, zs[q]), ss.at[j], rs.at[j], to)
+    def link(q, j, ss, rs, to):
+        return remote(at(c, j, zs[q]), at(c, j, zs[q]), ss.at[j], rs.at[j], to)
+
+    def hop1(j):
+        arrived(at(c, j, z1), r_h1.at[j])
+        cpy = link(1, j, s_h2, r_h2, pair)
         cpy.start()
         chain.append(cpy)
 
-    for j in range(5):
-        pass_on(0, j, s_h1, r_h1, outward)
-    for j in range(5):
-        share(0, j)
-
-    def hop1(j):
-        arrived(at(c, j, z1), r_h1.at[j])
-        pass_on(1, j, s_h2, r_h2, pair)
-        share(1, j)
+    third = []
+    fourth = []
 
     def hop2(j):
         arrived(at(c, j, z2), r_h2.at[j])
-        pass_on(2, j, s_h3, r_h3, outward)
-        share(2, j)
+        cpy = link(2, j, s_h3, r_h3, outward)
+        goes = side == (1 if j < 3 else 0)
+        third.append((goes, cpy))
+
+        @pl.when(goes)
+        def _():
+            cpy.start()
 
     def hop3(j):
-        arrived(at(c, j, z3), r_h3.at[j])
-        share(3, j)
+        cpy = link(3, j, s_h4, r_h4, pair)
+        comes = side == (0 if j < 3 else 1)
+        fourth.append((comes, cpy))
+
+        @pl.when(comes)
+        def _():
+            arrived(at(c, j, z3), r_h3.at[j])
+            cpy.start()
+
+        @pl.when(jnp.logical_not(comes))
+        def _():
+            arrived(at(c, j, z3), r_h4.at[j])
+
+    def own_slabs(first, count):
+        @pl.when(c == 0)
+        def _():
+            for j in range(first, first + count):
+                wall[j, rows(zh, SLAB), :] = packed(j)
+
+        @pl.when(c == 1)
+        def _():
+            for j in range(first, first + count):
+                if j == 0:
+                    w = jnp.concatenate([pland[k] for k in range(4)], axis=0)
+                else:
+                    w = packed(j - 1)
+                wall[5 + j, rows(zh, SLAB), :] = w
+
+        for j in range(first, first + count):
+            cpy = link(0, j, s_h1, r_h1, outward)
+            cpy.start()
+            chain.append(cpy)
+        share(0, first, count)
+
+    k1_forward(0)
+    wy_wait(0, 48)
+    for dx in range(1, 4):
+        arrived(pland.at[lax.rem(x - dx + 4, 4)], r_pr.at[dx - 1])
+    own_slabs(0, 2)
+    k1_forward(1)
 
     arrived(pxp, r_px)
     norm_rows(pxp, 1 + 8 * other)
@@ -270,6 +332,10 @@
     @pl.when(y == 3)
     def _():
         nb[:, 17] = jnp.zeros((2, 32, D), BF16)
+
+    wy_wait(48, 64)
+    own_slabs(2, 3)
+    k1_forward(2)
 
     col = lax.broadcasted_iota(jnp.int32, (D, 256), 1)
     row = lax.broadcasted_iota(jnp.int32, (D, 256), 0)
@@ -305,18 +371,18 @@
     hop1(0)
     hop1(1)
 
-    for dx in range(1, 4):
-        for q in range(3):
-            arrived(k1x.at[lax.rem(x - dx + 4, 4), pl.ds(3 * q, 3)], r_kx.at[dx - 1, q])
-    for t in range(9):
-        dy, dx = t // 3, t % 3
-        w = jnp.concatenate([k1x[k, t] for k in range(4)], axis=0)
-        a = bq[dx, dy % 2, :, pl.ds(dy // 2, 8), :, :].reshape(256, 256)[:, :160]
-        got = dot(a, w)
-        if t == 0:
-            acc1[...] = got
-        else:
-            acc1[...] += got
+    for q in range(3):
+        for d in range(1, 4):
+            arrived(k1x.at[lax.rem(line - d + 4, 4), pl.ds(3 * q, 3)], r_kx.at[d - 1, q])
+        for t in range(3 * q, 3 * q + 3):
+            dy, dx = t // 3, t % 3
+            w = jnp.concatenate([k1x[k, t] for k in range(4)], axis=0)
+            a = bq[dx, dy % 2, :, pl.ds(dy // 2, 8), :, :].reshape(256, 256)[:, :160]
+            got = dot(a, w)
+            if t == 0:
+                acc1[...] = got
+            else:
+                acc1[...] += got
     part[...] = acc1[...].astype(BF16)
     pa_copies = []
     for k in range(1, 4):
@@ -352,8 +418,8 @@
     core = lax.div(x, 2)
     slot = lax.rem(x, 2)
     pl_copies = []
-    for dx in range(4):
-        for dy in range(4):
+    for dx in (2, 1, 3, 0):
+        for dy in (2, 1, 3, 0):
             k = dx * 4 + dy
             cpy = remote(
                 pb, plin.at[slot, rows(ch, 64)], s_pl.at[k], r_pl.at[slot * 8 + ch],
@@ -365,7 +431,7 @@
 
     @pl.when(core != c)
     def _():
-        pl_copies[0].start()
+        pl_copies[-1].start()
 
     @pl.when(core == c)
     def _():
@@ -373,31 +439,38 @@
 
     for j in range(3, 5):
         hop1(j)
+    share(1, 0, 5)
     for j in range(5):
         hop2(j)
+    share(2, 0, 5)
     hop3(0)
-
-    for e in range(2):
-        for k in range(8):
-            own = jnp.logical_and(2 * c + e == x, ch == k)
-
-            @pl.when(jnp.logical_not(own))
-            def _(e=e, k=k):
-                arrived(plin.at[e, pl.ds(64 * k, 64)], r_pl.at[e * 8 + k])
-
-    @pl.when(c == 0)
-    def _():
-        for q in range(4):
-            arrived(at(1, 0, zs[q]), r_dd.at[q, 0])
+    share(3, 0, 1)
+
+    def shared(k):
+        q, j, n = shares[k]
+        arrived(wall.at[pl.ds(5 * other + j, n), rows(zs[q], SLAB)], r_dd.at[k])
+
+    for k in (0, 2, 3, 4):
+        shared(k)
 
     pn[...] = jnp.concatenate(
         [wall[5, pl.ds(zb * SLAB + xb * 40, 40), :] for xb in range(4) for zb in range(4)], axis=0
     )
-    gain, shift = g2[:, lanes(x)], s2[:, lanes(x)]
+    gain, shift = g2w[:, lanes(x)], s2w[:, lanes(x)]
     inside = lax.rem(lax.broadcasted_iota(jnp.int32, (128, 1), 0), 16) < 14
 
+    def nearest(i):
+        return lax.rem(y + i + jnp.where(i == 2, 1, 0) - jnp.where(i == 3, 1, 0), 4)
+
     def project(i, carry):
-        e, m = lax.div(i, 4), lax.rem(i, 4)
+        e, m = lax.rem(i, 2), nearest(lax.div(i, 2))
+        for k in range(2):
+            own = jnp.logical_and(2 * c + e == x, ch == 2 * m + k)
+
+            @pl.when(jnp.logical_not(own))
+            def _(k=k):
+                arrived(plin.at[e, rows(2 * m + k, 64)], r_pl.at[e * 8 + 2 * m + k])
+
         p = dot(plin[e, rows(m, 128), :], pn[...]).astype(BF16)
         pjb[e, rows(m, 128), :] = p
         v = jnp.maximum(p.astype(F32) * gain + shift, 0.0)
@@ -431,16 +504,9 @@
 
     for j in range(1, 5):
         hop3(j)
-    for q in range(4):
-        for j in range(5):
-            if j == 0:
-
-                @pl.when(c == 1)
-                def _(q=q):
-                    arrived(at(0, 0, zs[q]), r_dd.at[q, 0])
-
-            else:
-                arrived(at(other, j, zs[q]), r_dd.at[q, j])
+    share(3, 1, 4)
+    for k in (1, 5):
+        shared(k)
 
     adds = x == y
 
@@ -481,29 +547,34 @@
 
     lax.fori_loop(0, 4, second, 0)
 
-    f_copies = []
-    for yb in range(4):
+    def finish(i, carry):
+        yb = nearest(i)
         total = jnp.zeros((64, D), F32)
         for xb in range(4):
             own = jnp.logical_and(jnp.logical_and(core == c, xb == x), yb == y)
 
             @pl.when(jnp.logical_not(own))
-            def _(xb=xb, yb=yb):
+            def _(xb=xb):
                 arrived(cin.at[xb * 4 + yb], r_c.at[xb * 4 + yb])
 
             total += cin[xb * 4 + yb].astype(F32)
-        columns = pl.ds(yb * D, D)
-        fb[:, columns] = total.astype(BF16)
-        cpy = remote(fb.at[:, columns], out.at[0, :, columns], s_f.at[yb], r_f.at[yb], pair)
-        f_copies.append(cpy)
+        fb[:, lanes(yb)] = total.astype(BF16)
 
         @pl.when(s == 0)
-        def _(cpy=cpy):
-            cpy.start()
+        def _():
+            f_copy(yb).start()
 
         @pl.when(s == 1)
-        def _(columns=columns):
-            out[1, :, columns] = fb[:, columns]
+        def _():
+            out[1, :, lanes(yb)] = fb[:, lanes(yb)]
+
+        return carry
+
+    def f_copy(yb):
+        block = fb.at[:, lanes(yb)]
+        return remote(block, out.at[0, :, lanes(yb)], s_f.at[yb], r_f.at[yb], pair)
+
+    lax.fori_loop(0, 4, finish, 0)
 
     @pl.when(s == 0)
     def _():
@@ -515,8 +586,8 @@
                 def _(sb=sb, xb=xb):
                     arrived(out.at[sb, :, pl.ds(xb * D, D)], r_pj.at[4 * sb + xb])
 
-        for cpy in f_copies:
-            cpy.wait_send()
+        for yb in range(4):
+            f_copy(yb).wait_send()
 
     @pl.when(s == 1)
     def _():
@@ -550,14 +621,26 @@
 
     @pl.when(k1_sends)
     def _():
-        for cpy in k1_copies:
+        for cpy in k1_copies[0]:
             cpy.wait_send()
 
+    @pl.when(diagonal)
+    def _():
+        for line_copies in k1_copies:
+            for cpy in line_copies:
+                cpy.wait_send()
+
+    for goes, cpy in third + fourth:
+
+        @pl.when(goes)
+        def _(cpy=cpy):
+            cpy.wait_send()
+
     @pl.when(core != c)
     def _():
-        pl_copies[0].wait_send()
-
-    for cpy in pr_copies + wy_copies + kx_copies + chain + pa_copies + pl_copies[1:]:
+        pl_copies[-1].wait_send()
+
+    for cpy in pr_copies + wy_copies + kx_copies + chain + pa_copies + pl_copies[:-1]:
         cpy.wait_send()
 
 
@@ -577,8 +660,8 @@
         return pltpu.VMEM(shape, dtype)
 
     counts = [
-        (), (), (2,), (), (2,), (), (3,), (3,), (3, 3), (3, 3), (3,), (3,), (8,), (8,),
-        (5,), (5,), (5,), (5,), (5,), (5,), (4, 5), (4, 5), (3,), (3,), (16,), (16,),
+        (), (), (2,), (), (2,), (), (4, 3), (3,), (3, 3), (3, 3), (3,), (3,), (16,), (16,),
+        (5,), (5,), (5,), (5,), (5,), (5,), (5,), (5,), (6,), (6,), (3,), (3,), (16,), (16,),
         (4,), (8,), (16,), (16,), (4,), (4,),
     ]
     result = pl.pallas_call(
@@ -612,6 +695,8 @@
             vmem(2, 512, D),
             vmem(16, 64, D),
             vmem(64, 4 * D),
+            vmem(1, 4 * D, dtype=F32),
+            vmem(1, 4 * D, dtype=F32),
         ]
         + [dma(n) for n in counts],
         compiler_params=pltpu.CompilerParams(
@@ -620,12 +705,12 @@
         cost_estimate=pl.CostEstimate(flops=8 * 10**9, bytes_accessed=10**7, transcendentals=0),
     )(
         pixels,
-        first_gain[None],
-        first_shift[None],
+        first_gain,
+        first_shift,
         first_kernel.reshape(9, 40, D),
         projection,
-        second_gain[None],
-        second_shift[None],
+        second_gain,
+        second_shift,
         second_kernel.reshape(9, 20, 4 * D),
     )
     return result.reshape(2, 4, 16, 4 * D)[None, :, :, :14]

time: 124 us -> 156 us (1.26)
  Pallas kernels: 113 us -> 151 us
  local copies, waits for them, and re-layouts: 9.48 us -> 4.31 us
    pallas_call x1, Pallas kernels: 113 us -> 151 us  [body(): pl.pallas_call(kernel, name='window', out_shape=jax.ShapeDtypeStruct((2,...]
    broadcast_in_dim x4 -> x0, local copies, waits for them, and re-layouts: 5.17 us -> none  [the longest x1 1.31 us: body(): second_gain[None]]
where the time goes in v2:
time: 156 us
  Pallas kernels  151 us (97%)
  local copies, waits for them, and re-layouts  4.31 us (3%)
    pallas_call x1, Pallas kernels, body(): pl.pallas_call(kernel, name='window', out_shape=jax.ShapeDtypeStruct((2,...  151 us
    unnamed x2, local copies, waits for them, and re-layouts  4.31 us

profile of v2, /device:TPU:59, one launch (start us, length us, event | category | flops | bytes accessed | tf_op | source)
XLA Modules:
  0.0 155.6 jit_solution(16349388123735416972)
XLA Ops:
  0.0 2.0 %copy.9.pix = bf16[2,8,28,640]{3,2,1,0:T(8,128)(2,1)} copy(bf16[2,8,28,640]{3,1,2,0:T(8,128)(2,1)} %param.8) | data formatting | bytes 1146880 | tf_op args[0]
  2.0 151.3 %window.1 = bf16[2,64,2560]{2,1,0:T(8,128)(2,1)} custom-call(bf16[2,8,28,640]{3,2,1,0:T(8,128)(2,1)} %copy.9.pix, f32[640]{0:T(1024)} %g1.1, f32[640]{0:T(1024)} %s1_.1, bf16[9,40,640]{2,1,0:T(8,128)(2,1)} %bitcast.9, bf16[40,2560]{1,0:T(8,128)(2,1)} %pr.1, f32[2560]{0:T(1024)} %g2.1, f32[2560]{0:T(1024)} %s2_.1, bf16[9,20,2560]{2,1,0:T(8,128)(2,1)} %bitcast.8), custom_call_target="tpu_custom_call" | custom-call | flops 8000000000 | bytes 10000000 | tf_op jit(solution)/shard_map/window/pallas_call | solution.py:667
  153.2 2.3 %copy.13 = bf16[2,4,14,2560]{3,1,2,0:T(4,128)(2,1)} copy(bf16[2,4,14,2560]{3,2,1,0:T(8,128)(2,1)} %bitcast.7) | data formatting | bytes 1146880

commit v3 on v2

--- a/solution.py
+++ b/solution.py
@@ -12,6 +12,9 @@
 SLAB = 160
 
 
+PARTS = ((pl.ds(0, 48), pl.ds(0, 48)), (pl.ds(48, 32), pl.ds(48, 64)))
+
+
 def lanes(i):
     return pl.ds(pl.multiple_of(i * D, 128), D)
 
@@ -28,7 +31,7 @@
     pix, g1, s1, k1, pr, g2, s2, k2,
     out,
     pxp, hal_t, hal_b, wp, wy, pland, wall, pn, k1x, nb, nsel, bq, acc1, part, prx, rtmp,
-    pb, plin, pjb, abuf, acc2, cp, cin, fb, g2w, s2w,
+    pb, plin, pjb, abuf, cp, cin, fb, g2w, s2w,
     s_px, r_px, s_ht, r_ht, s_hb, r_hb, s_k1, r_k1, s_kx, r_kx, s_pr, r_pr, s_wy, r_wy,
     s_h1, r_h1, s_h2, r_h2, s_h3, r_h3, s_h4, r_h4, s_dd, r_dd, s_pa, r_pa, s_pl, r_pl,
     s_pj, r_pj, s_c, r_c, s_f, r_f,
@@ -70,14 +73,7 @@
     met.append(dev(1 - s, x, zh + 2, y, c))
     for to in met:
         pl.semaphore_signal(barrier, inc=1, device_id=to, device_id_type=MESH)
-    diagonal = jnp.logical_and(c == 1, x == y)
-
-    @pl.when(jnp.logical_and(c == 1, x != y))
-    def _():
-        to = dev(1 - s, y, zh - (1 - s) + 2 * s, y, c)
-        pl.semaphore_signal(barrier, inc=1, device_id=to, device_id_type=MESH)
-
-    pl.semaphore_wait(barrier, len(met) + jnp.where(diagonal, 3, 0))
+    pl.semaphore_wait(barrier, len(met))
 
     px_copy = remote(pix, pxp, s_px, r_px, partner)
     px_copy.start()
@@ -105,29 +101,21 @@
     zq_off = (1 - s) * 3 * c + s * (1 + c)
     zq = lax.rem(zh + zq_off, 4)
     line = jnp.where(c == 0, x, y)
+    diagonal = jnp.logical_and(c == 1, x == y)
     k1_gets = jnp.logical_not(jnp.logical_and(s == 0, c == 0))
-    k1_sends = jnp.logical_and(c == 0, s == 0)
+    k1_sends = jnp.logical_or(jnp.logical_and(c == 0, s == 0), diagonal)
     k1_copies = [
-        [
-            remote(
-                k1.at[pl.ds(3 * q, 3)], k1x.at[line, pl.ds(3 * q, 3)], s_k1.at[dx, q], r_k1.at[q],
-                dev(1 - s, x + dx, zh + s - (1 - s) * (1 + c), y, c),
-            )
-            for q in range(3)
-        ]
-        for dx in range(4)
+        remote(
+            k1.at[pl.ds(3 * q, 3)], k1x.at[line, pl.ds(3 * q, 3)], s_k1.at[0, q], r_k1.at[q],
+            dev(1 - s, x, zh + s - (1 - s) * (1 + c), y, c),
+        )
+        for q in range(3)
     ]
 
     @pl.when(k1_sends)
     def _():
-        for cpy in k1_copies[0]:
+        for cpy in k1_copies:
             cpy.start()
-
-    @pl.when(diagonal)
-    def _():
-        for q in range(3):
-            for dx in (2, 1, 3, 0):
-                k1_copies[dx][q].start()
 
     @pl.when(jnp.logical_not(k1_gets))
     def _():
@@ -144,29 +132,34 @@
     pland[x] = pr[:, lanes(x)]
 
     wy_copies = []
-    for part_at, size, taps in ((0, 48, (0, 1)), (48, 64, (2, 3, 4))):
-        for half, first, count in ((0, 0, 5), (1, 5, 4)):
-            used = 0
-            for a in taps:
+    for lower in range(2):
+        for half, first, count in ((0, 0, 4), (1, 4, 5)):
+            for a in range(3 * lower, 3 + 2 * lower):
                 if a < count:
-                    wp[half, pl.ds(part_at + used, 20), :] = k2[first + a]
-                    used += 20
-            blank = size - used
-            wp[half, pl.ds(part_at + used, blank), :] = jnp.zeros((blank, 4 * D), BF16)
+                    wp[half, pl.ds(20 * a, 20), :] = k2[first + a]
+            if half and lower:
+                wp[1, pl.ds(100, 12), :] = jnp.zeros((12, 4 * D), BF16)
         for dy in (2, 1, 3, 0):
             for dc in range(2):
                 if dy == 0 and dc == 0:
                     continue
                 ty = lax.rem(y + dy, 4)
                 tc = c if dc == 0 else other
-                k = (part_at // 48) * 8 + dy * 2 + dc
-                cpy = remote(
-                    wp.at[tc, pl.ds(part_at, size), lanes(ty)], wy.at[ch, pl.ds(part_at, size)],
-                    s_wy.at[k], r_wy.at[k], dev(s, x, zh, ty, tc),
-                )
-                cpy.start()
-                wy_copies.append(cpy)
-    wy[ch] = wp[c, :, lanes(y)]
+                k = lower * 8 + dy * 2 + dc
+                for core in range(2):
+                    part_rows = PARTS[lower][core]
+                    cpy = remote(
+                        wp.at[core, part_rows, lanes(ty)], wy.at[ch, part_rows],
+                        s_wy.at[k], r_wy.at[k], dev(s, x, zh, ty, core),
+                    )
+                    wy_copies.append((tc == core, cpy))
+
+                    @pl.when(tc == core)
+                    def _(cpy=cpy):
+                        cpy.start()
+
+    wy[ch, pl.ds(0, 80), :] = wp[c, pl.ds(0, 80), lanes(y)]
+    wy[ch, pl.ds(80, 32), :] = wp[1, pl.ds(80, 32), lanes(y)]
 
     g2w[...] = g2[...].reshape(1, 4 * D)
     s2w[...] = s2[...].reshape(1, 4 * D)
@@ -191,13 +184,8 @@
 
     norm_rows(pix, 1 + 8 * c)
 
-    for i in range(4):
-        both = pix[s, 2 * i].astype(F32) + pix[s, 2 * i + 1].astype(F32)
-        both = jnp.concatenate([both, jnp.zeros((4, D), F32)], axis=0)
-        for b in range(5):
-            rtmp[i, b] = both[:, 128 * b : 128 * b + 128]
-
     kx_copies = []
+    diagonal_copies = []
 
     def k1_forward(q):
         block = k1x.at[line, pl.ds(3 * q, 3)]
@@ -205,6 +193,17 @@
         @pl.when(k1_gets)
         def _():
             arrived(block, r_k1.at[q])
+
+        across = [
+            remote(block, block, s_k1.at[d, q], r_k1.at[q], dev(s, x + d, zh, y, c))
+            for d in (2, 1, 3)
+        ]
+        diagonal_copies.extend(across)
+
+        @pl.when(diagonal)
+        def _():
+            for cpy in across:
+                cpy.start()
 
         for d in (2, 1, 3):
             cpy = remote(
@@ -214,18 +213,23 @@
             cpy.start()
             kx_copies.append(cpy)
 
-    def wy_wait(part_at, size):
-        for dy in range(4):
-            for dc in range(2):
-                if dy or dc:
-                    sy = lax.rem(y - dy + 4, 4)
-                    sc = c if dc == 0 else other
-                    k = (part_at // 48) * 8 + dy * 2 + dc
-                    arrived(wy.at[sy * 2 + sc, pl.ds(part_at, size)], r_wy.at[k])
+    def wy_wait(lower):
+        for core in range(2):
+
+            @pl.when(c == core)
+            def _(core=core):
+                for dy in range(4):
+                    for dc in range(2):
+                        if dy or dc:
+                            sy = lax.rem(y - dy + 4, 4)
+                            sc = core if dc == 0 else 1 - core
+                            arrived(
+                                wy.at[sy * 2 + sc, PARTS[lower][core]],
+                                r_wy.at[lower * 8 + dy * 2 + dc],
+                            )
 
     def packed(a):
-        at_row = 20 * a if a < 2 else 48 + 20 * (a - 2)
-        return jnp.concatenate([wy[k, pl.ds(at_row, 20), :] for k in range(8)], axis=0)
+        return jnp.concatenate([wy[k, pl.ds(20 * a, 20), :] for k in range(8)], axis=0)
 
     def at(core, j, z_):
         return wall.at[5 * core + j, rows(z_, SLAB)]
@@ -261,7 +265,7 @@
     def hop2(j):
         arrived(at(c, j, z2), r_h2.at[j])
         cpy = link(2, j, s_h3, r_h3, outward)
-        goes = side == (1 if j < 3 else 0)
+        goes = side >= 0
         third.append((goes, cpy))
 
         @pl.when(goes)
@@ -270,7 +274,7 @@
 
     def hop3(j):
         cpy = link(3, j, s_h4, r_h4, pair)
-        comes = side == (0 if j < 3 else 1)
+        comes = side < 0
         fourth.append((comes, cpy))
 
         @pl.when(comes)
@@ -278,24 +282,23 @@
             arrived(at(c, j, z3), r_h3.at[j])
             cpy.start()
 
-        @pl.when(jnp.logical_not(comes))
-        def _():
-            arrived(at(c, j, z3), r_h4.at[j])
+    def hop4(j):
+        arrived(at(c, j, z3), r_h3.at[j])
 
     def own_slabs(first, count):
         @pl.when(c == 0)
-        def _():
-            for j in range(first, first + count):
-                wall[j, rows(zh, SLAB), :] = packed(j)
-
-        @pl.when(c == 1)
         def _():
             for j in range(first, first + count):
                 if j == 0:
                     w = jnp.concatenate([pland[k] for k in range(4)], axis=0)
                 else:
                     w = packed(j - 1)
-                wall[5 + j, rows(zh, SLAB), :] = w
+                wall[j, rows(zh, SLAB), :] = w
+
+        @pl.when(c == 1)
+        def _():
+            for j in range(first, first + count):
+                wall[5 + j, rows(zh, SLAB), :] = packed(j)
 
         for j in range(first, first + count):
             cpy = link(0, j, s_h1, r_h1, outward)
@@ -303,39 +306,35 @@
             chain.append(cpy)
         share(0, first, count)
 
+    arrived(pxp, r_px)
+    norm_rows(pxp, 1 + 8 * other)
+
+    @pl.when(y > 0)
+    def _():
+        arrived(hal_t, r_ht)
+        for e in range(2):
+            nb[e, 0] = norm(hal_t[e, 0])
+
+    @pl.when(y == 0)
+    def _():
+        nb[:, 0] = jnp.zeros((2, 32, D), BF16)
+
+    @pl.when(y < 3)
+    def _():
+        arrived(hal_b, r_hb)
+        for e in range(2):
+            nb[e, 17] = norm(hal_b[e, 0])
+
+    @pl.when(y == 3)
+    def _():
+        nb[:, 17] = jnp.zeros((2, 32, D), BF16)
+
     k1_forward(0)
-    wy_wait(0, 48)
+    wy_wait(0)
     for dx in range(1, 4):
         arrived(pland.at[lax.rem(x - dx + 4, 4)], r_pr.at[dx - 1])
     own_slabs(0, 2)
     k1_forward(1)
-
-    arrived(pxp, r_px)
-    norm_rows(pxp, 1 + 8 * other)
-
-    @pl.when(y > 0)
-    def _():
-        arrived(hal_t, r_ht)
-        for e in range(2):
-            nb[e, 0] = norm(hal_t[e, 0])
-
-    @pl.when(y == 0)
-    def _():
-        nb[:, 0] = jnp.zeros((2, 32, D), BF16)
-
-    @pl.when(y < 3)
-    def _():
-        arrived(hal_b, r_hb)
-        for e in range(2):
-            nb[e, 17] = norm(hal_b[e, 0])
-
-    @pl.when(y == 3)
-    def _():
-        nb[:, 17] = jnp.zeros((2, 32, D), BF16)
-
-    wy_wait(48, 64)
-    own_slabs(2, 3)
-    k1_forward(2)
 
     col = lax.broadcasted_iota(jnp.int32, (D, 256), 1)
     row = lax.broadcasted_iota(jnp.int32, (D, 256), 0)
@@ -351,6 +350,7 @@
         return carry
 
     lax.fori_loop(0, 6, select_rows, 0)
+    k1_forward(2)
 
     def box(i, carry):
         e, r = lax.div(i, 9), lax.rem(i, 9)
@@ -367,11 +367,13 @@
         return carry
 
     lax.fori_loop(0, 18, box, 0)
-
+    wy_wait(1)
+    own_slabs(2, 3)
     hop1(0)
-    hop1(1)
 
     for q in range(3):
+        if q == 2:
+            hop1(1)
         for d in range(1, 4):
             arrived(k1x.at[lax.rem(line - d + 4, 4), pl.ds(3 * q, 3)], r_kx.at[d - 1, q])
         for t in range(3 * q, 3 * q + 3):
@@ -394,7 +396,14 @@
         )
         cpy.start()
         pa_copies.append(cpy)
+    for i in range(4):
+        both = pix[s, 2 * i].astype(F32) + pix[s, 2 * i + 1].astype(F32)
+        both = jnp.concatenate([both, jnp.zeros((4, D), F32)], axis=0)
+        for b in range(5):
+            rtmp[i, b] = both[:, 128 * b : 128 * b + 128]
+
     hop1(2)
+    hop2(0)
     for k in range(3):
         arrived(prx.at[k], r_pa.at[k])
     total = acc1[rows(s * 2 + c, 64), :]
@@ -437,13 +446,16 @@
     def _():
         plin[slot, rows(ch, 64), :] = pb[...]
 
-    for j in range(3, 5):
-        hop1(j)
+    hop1(3)
+    hop2(1)
+    hop1(4)
     share(1, 0, 5)
-    for j in range(5):
+    for j in range(2, 5):
         hop2(j)
     share(2, 0, 5)
-    hop3(0)
+    for j in range(5):
+        hop3(j)
+    hop4(0)
     share(3, 0, 1)
 
     def shared(k):
@@ -454,7 +466,7 @@
         shared(k)
 
     pn[...] = jnp.concatenate(
-        [wall[5, pl.ds(zb * SLAB + xb * 40, 40), :] for xb in range(4) for zb in range(4)], axis=0
+        [wall[0, pl.ds(zb * SLAB + xb * 40, 40), :] for xb in range(4) for zb in range(4)], axis=0
     )
     gain, shift = g2w[:, lanes(x)], s2w[:, lanes(x)]
     inside = lax.rem(lax.broadcasted_iota(jnp.int32, (128, 1), 0), 16) < 14
@@ -503,7 +515,7 @@
                 out[0, :, lanes(x)] = src[...]
 
     for j in range(1, 5):
-        hop3(j)
+        hop4(j)
     share(3, 1, 4)
     for k in (1, 5):
         shared(k)
@@ -521,16 +533,16 @@
 
     def second(i, carry):
         e, m = lax.div(i, 2), lax.rem(i, 2)
-        for t in range(9):
-            dy, dx = t // 3, t % 3
-            a = abuf[dx, e, pl.ds(pl.multiple_of(256 * m + 16 * dy, 16), 256), :]
-            got = dot(a, wall[t if t < 5 else t + 1])
-            if t == 0:
-                acc2[...] = got
-            else:
-                acc2[...] += got
+        a = jnp.concatenate(
+            [
+                abuf[t % 3, e, pl.ds(pl.multiple_of(256 * m + 16 * (t // 3), 16), 256), :]
+                for t in range(9)
+            ],
+            axis=1,
+        )
+        total = dot(a, wall[pl.ds(1, 9)].reshape(9 * D, D))
         proj = pjb[e, rows(m, 256), :].astype(F32)
-        cp[e, rows(m, 256), :] = (acc2[...] + jnp.where(adds, proj, 0.0)).astype(BF16)
+        cp[e, rows(m, 256), :] = (total + jnp.where(adds, proj, 0.0)).astype(BF16)
         for q in range(4):
             k = 4 * m + q
             own = c_own(e, k)
@@ -621,16 +633,15 @@
 
     @pl.when(k1_sends)
     def _():
-        for cpy in k1_copies[0]:
+        for cpy in k1_copies:
             cpy.wait_send()
 
     @pl.when(diagonal)
     def _():
-        for line_copies in k1_copies:
-            for cpy in line_copies:
-                cpy.wait_send()
-
-    for goes, cpy in third + fourth:
+        for cpy in diagonal_copies:
+            cpy.wait_send()
+
+    for goes, cpy in wy_copies + third + fourth:
 
         @pl.when(goes)
         def _(cpy=cpy):
@@ -640,7 +651,7 @@
     def _():
         pl_copies[-1].wait_send()
 
-    for cpy in pr_copies + wy_copies + kx_copies + chain + pa_copies + pl_copies[:-1]:
+    for cpy in pr_copies + kx_copies + chain + pa_copies + pl_copies[:-1]:
         cpy.wait_send()
 
 
@@ -691,7 +702,6 @@
             vmem(2, 512, D),
             vmem(2, 512, D),
             vmem(3, 2, 544, D),
-            vmem(256, D, dtype=F32),
             vmem(2, 512, D),
             vmem(16, 64, D),
             vmem(64, 4 * D),

time: 156 us -> 113 us (0.72)
  the two profiles are of different devices: /device:TPU:59 before, /device:TPU:63 now
where the time goes in v3:
time: 113 us
  Pallas kernels  108 us (96%)
  local copies, waits for them, and re-layouts  4.31 us (4%)
    pallas_call x1, Pallas kernels, body(): pl.pallas_call(kernel, name='window', out_shape=jax.ShapeDtypeStruct((2,...  108 us
    unnamed x2, local copies, waits for them, and re-layouts  4.31 us

profile of v3, /device:TPU:63, one launch (start us, length us, event | category | flops | bytes accessed | tf_op | source)
XLA Modules:
  0.0 112.6 jit_solution(16769637011876536155)
XLA Ops:
  0.0 2.0 %copy.9.pix = bf16[2,8,28,640]{3,2,1,0:T(8,128)(2,1)} copy(bf16[2,8,28,640]{3,1,2,0:T(8,128)(2,1)} %param.8) | data formatting | bytes 1146880 | tf_op args[0]
  2.0 108.3 %window.1 = bf16[2,64,2560]{2,1,0:T(8,128)(2,1)} custom-call(bf16[2,8,28,640]{3,2,1,0:T(8,128)(2,1)} %copy.9.pix, f32[640]{0:T(1024)} %g1.1, f32[640]{0:T(1024)} %s1_.1, bf16[9,40,640]{2,1,0:T(8,128)(2,1)} %bitcast.9, bf16[40,2560]{1,0:T(8,128)(2,1)} %pr.1, f32[2560]{0:T(1024)} %g2.1, f32[2560]{0:T(1024)} %s2_.1, bf16[9,20,2560]{2,1,0:T(8,128)(2,1)} %bitcast.8), custom_call_target="tpu_custom_call" | custom-call | flops 8000000000 | bytes 10000000 | tf_op jit(solution)/shard_map/window/pallas_call | solution.py:678
  110.3 2.3 %copy.13 = bf16[2,4,14,2560]{3,1,2,0:T(4,128)(2,1)} copy(bf16[2,4,14,2560]{3,2,1,0:T(8,128)(2,1)} %bitcast.7) | data formatting | bytes 1146880

commit v4 on v3

--- a/solution.py
+++ b/solution.py
@@ -532,7 +532,8 @@
         return jnp.logical_and(2 * c + e == x, k == ch)
 
     def second(i, carry):
-        e, m = lax.div(i, 2), lax.rem(i, 2)
+        e = lax.rem(lax.div(i, 2) + x, 2)
+        m = lax.rem(i + 1 + lax.div(y, 2), 2)
         a = jnp.concatenate(
             [
                 abuf[t % 3, e, pl.ds(pl.multiple_of(256 * m + 16 * (t // 3), 16), 256), :]
@@ -560,7 +561,9 @@
     lax.fori_loop(0, 4, second, 0)
 
     def finish(i, carry):
-        yb = nearest(i)
+        far = 2 * (1 - lax.div(y, 2)) + i
+        near = jnp.where(i == 3, y, y + 1 - 2 * lax.rem(y, 2))
+        yb = jnp.where(i < 2, far, near)
         total = jnp.zeros((64, D), F32)
         for xb in range(4):
             own = jnp.logical_and(jnp.logical_and(core == c, xb == x), yb == y)

time: 113 us -> 107 us (0.947)
  the two profiles are of different devices: /device:TPU:63 before, /device:TPU:59 now
where the time goes in v4:
time: 107 us; the launch traced here: 105 us
  Pallas kernels  101 us (94%)
  local copies, waits for them, and re-layouts  4.31 us (4%)
    pallas_call x1, Pallas kernels, body(): pl.pallas_call(kernel, name='window', out_shape=jax.ShapeDtypeStruct((2,...  101 us
    unnamed x2, local copies, waits for them, and re-layouts  4.31 us

profile of v4, /device:TPU:59, one launch (start us, length us, event | category | flops | bytes accessed | tf_op | source)
XLA Modules:
  0.0 105.3 jit_solution(10822404639571710596)
XLA Ops:
  0.0 2.0 %copy.9.pix = bf16[2,8,28,640]{3,2,1,0:T(8,128)(2,1)} copy(bf16[2,8,28,640]{3,1,2,0:T(8,128)(2,1)} %param.8) | data formatting | bytes 1146880 | tf_op args[0]
  2.0 101.0 %window.1 = bf16[2,64,2560]{2,1,0:T(8,128)(2,1)} custom-call(bf16[2,8,28,640]{3,2,1,0:T(8,128)(2,1)} %copy.9.pix, f32[640]{0:T(1024)} %g1.1, f32[640]{0:T(1024)} %s1_.1, bf16[9,40,640]{2,1,0:T(8,128)(2,1)} %bitcast.9, bf16[40,2560]{1,0:T(8,128)(2,1)} %pr.1, f32[2560]{0:T(1024)} %g2.1, f32[2560]{0:T(1024)} %s2_.1, bf16[9,20,2560]{2,1,0:T(8,128)(2,1)} %bitcast.8), custom_call_target="tpu_custom_call" | custom-call | flops 8000000000 | bytes 10000000 | tf_op jit(solution)/shard_map/window/pallas_call | solution.py:681
  103.0 2.3 %copy.13 = bf16[2,4,14,2560]{3,1,2,0:T(4,128)(2,1)} copy(bf16[2,4,14,2560]{3,2,1,0:T(8,128)(2,1)} %bitcast.7) | data formatting | bytes 1146880

commit v5 on v4

--- a/solution.py
+++ b/solution.py
@@ -73,30 +73,11 @@
     met.append(dev(1 - s, x, zh + 2, y, c))
     for to in met:
         pl.semaphore_signal(barrier, inc=1, device_id=to, device_id_type=MESH)
+    for half, first, count in ((0, 0, 4), (1, 4, 5)):
+        for a in range(count):
+            wp[half, pl.ds(20 * a, 20), :] = k2[first + a]
+    wp[1, pl.ds(100, 12), :] = jnp.zeros((12, 4 * D), BF16)
     pl.semaphore_wait(barrier, len(met))
-
-    px_copy = remote(pix, pxp, s_px, r_px, partner)
-    px_copy.start()
-    down = [
-        remote(pix.at[:, pl.ds(7, 1)], hal_t, s_ht.at[k], r_ht, dev(s, x, zh, y + 1, k))
-        for k in range(2)
-    ]
-    up = [
-        remote(pix.at[:, pl.ds(0, 1)], hal_b, s_hb.at[k], r_hb, dev(s, x, zh, y - 1, k))
-        for k in range(2)
-    ]
-    sends_down = jnp.logical_and(c == 1, y < 3)
-    sends_up = jnp.logical_and(c == 0, y > 0)
-
-    @pl.when(sends_down)
-    def _():
-        for cpy in down:
-            cpy.start()
-
-    @pl.when(sends_up)
-    def _():
-        for cpy in up:
-            cpy.start()
 
     zq_off = (1 - s) * 3 * c + s * (1 + c)
     zq = lax.rem(zh + zq_off, 4)
@@ -121,6 +102,29 @@
     def _():
         k1x[x] = k1[...]
 
+    px_copy = remote(pix, pxp, s_px, r_px, partner)
+    px_copy.start()
+    down = [
+        remote(pix.at[:, pl.ds(7, 1)], hal_t, s_ht.at[k], r_ht, dev(s, x, zh, y + 1, k))
+        for k in range(2)
+    ]
+    up = [
+        remote(pix.at[:, pl.ds(0, 1)], hal_b, s_hb.at[k], r_hb, dev(s, x, zh, y - 1, k))
+        for k in range(2)
+    ]
+    sends_down = jnp.logical_and(c == 1, y < 3)
+    sends_up = jnp.logical_and(c == 0, y > 0)
+
+    @pl.when(sends_down)
+    def _():
+        for cpy in down:
+            cpy.start()
+
+    @pl.when(sends_up)
+    def _():
+        for cpy in up:
+            cpy.start()
+
     pr_copies = []
     for dx in range(1, 4):
         to = lax.rem(x + dx, 4)
@@ -133,12 +137,6 @@
 
     wy_copies = []
     for lower in range(2):
-        for half, first, count in ((0, 0, 4), (1, 4, 5)):
-            for a in range(3 * lower, 3 + 2 * lower):
-                if a < count:
-                    wp[half, pl.ds(20 * a, 20), :] = k2[first + a]
-            if half and lower:
-                wp[1, pl.ds(100, 12), :] = jnp.zeros((12, 4 * D), BF16)
         for dy in (2, 1, 3, 0):
             for dc in range(2):
                 if dy == 0 and dc == 0:

time: 107 us -> 107 us (level)
  no operation moved by 1% of the time
where the time goes in v5:
time: 107 us; the launch traced here: 105 us
  Pallas kernels  101 us (94%)
  local copies, waits for them, and re-layouts  4.31 us (4%)
    pallas_call x1, Pallas kernels, body(): pl.pallas_call(kernel, name='window', out_shape=jax.ShapeDtypeStruct((2,...  101 us
    unnamed x2, local copies, waits for them, and re-layouts  4.31 us

profile of v5, /device:TPU:59, one launch (start us, length us, event | category | flops | bytes accessed | tf_op | source)
XLA Modules:
  0.0 105.3 jit_solution(3478263606121666395)
XLA Ops:
  0.0 2.0 %copy.9.pix = bf16[2,8,28,640]{3,2,1,0:T(8,128)(2,1)} copy(bf16[2,8,28,640]{3,1,2,0:T(8,128)(2,1)} %param.8) | data formatting | bytes 1146880 | tf_op args[0]
  2.0 101.0 %window.1 = bf16[2,64,2560]{2,1,0:T(8,128)(2,1)} custom-call(bf16[2,8,28,640]{3,2,1,0:T(8,128)(2,1)} %copy.9.pix, f32[640]{0:T(1024)} %g1.1, f32[640]{0:T(1024)} %s1_.1, bf16[9,40,640]{2,1,0:T(8,128)(2,1)} %bitcast.9, bf16[40,2560]{1,0:T(8,128)(2,1)} %pr.1, f32[2560]{0:T(1024)} %g2.1, f32[2560]{0:T(1024)} %s2_.1, bf16[9,20,2560]{2,1,0:T(8,128)(2,1)} %bitcast.8), custom_call_target="tpu_custom_call" | custom-call | flops 8000000000 | bytes 10000000 | tf_op jit(solution)/shard_map/window/pallas_call | solution.py:679
  103.0 2.3 %copy.13 = bf16[2,4,14,2560]{3,1,2,0:T(4,128)(2,1)} copy(bf16[2,4,14,2560]{3,2,1,0:T(8,128)(2,1)} %bitcast.7) | data formatting | bytes 1146880

commit v6 on v3

--- a/solution.py
+++ b/solution.py
@@ -531,20 +531,26 @@
     def c_own(e, k):
         return jnp.logical_and(2 * c + e == x, k == ch)
 
+    def from_far(i, sign):
+        step = 2 - i + jnp.where(i >= 2, 3 * (3 - i) , 0)
+        step = jnp.where(i == 3, 0, step)
+        return lax.rem(y + sign * step + 4, 4)
+
     def second(i, carry):
-        e, m = lax.div(i, 2), lax.rem(i, 2)
+        e = lax.rem(lax.div(i, 4) + x, 2)
+        m = from_far(lax.rem(i, 4), 1)
         a = jnp.concatenate(
             [
-                abuf[t % 3, e, pl.ds(pl.multiple_of(256 * m + 16 * (t // 3), 16), 256), :]
+                abuf[t % 3, e, pl.ds(pl.multiple_of(128 * m + 16 * (t // 3), 16), 128), :]
                 for t in range(9)
             ],
             axis=1,
         )
         total = dot(a, wall[pl.ds(1, 9)].reshape(9 * D, D))
-        proj = pjb[e, rows(m, 256), :].astype(F32)
-        cp[e, rows(m, 256), :] = (total + jnp.where(adds, proj, 0.0)).astype(BF16)
-        for q in range(4):
-            k = 4 * m + q
+        proj = pjb[e, rows(m, 128), :].astype(F32)
+        cp[e, rows(m, 128), :] = (total + jnp.where(adds, proj, 0.0)).astype(BF16)
+        for q in range(2):
+            k = 2 * m + q
             own = c_own(e, k)
 
             @pl.when(jnp.logical_not(own))
@@ -557,10 +563,10 @@
 
         return carry
 
-    lax.fori_loop(0, 4, second, 0)
+    lax.fori_loop(0, 8, second, 0)
 
     def finish(i, carry):
-        yb = nearest(i)
+        yb = from_far(i, -1)
         total = jnp.zeros((64, D), F32)
         for xb in range(4):
             own = jnp.logical_and(jnp.logical_and(core == c, xb == x), yb == y)

time: 113 us -> 103 us (0.912)
  the two profiles are of different devices: /device:TPU:63 before, /device:TPU:59 now
where the time goes in v6:
time: 103 us; the launch traced here: 102 us
  Pallas kernels  97.5 us (95%)
  local copies, waits for them, and re-layouts  4.31 us (4%)
    pallas_call x1, Pallas kernels, body(): pl.pallas_call(kernel, name='window', out_shape=jax.ShapeDtypeStruct((2,...  97.5 us
    unnamed x2, local copies, waits for them, and re-layouts  4.31 us

profile of v6, /device:TPU:59, one launch (start us, length us, event | category | flops | bytes accessed | tf_op | source)
XLA Modules:
  0.0 101.9 jit_solution(9694261060853177614)
XLA Ops:
  0.0 2.0 %copy.9.pix = bf16[2,8,28,640]{3,2,1,0:T(8,128)(2,1)} copy(bf16[2,8,28,640]{3,1,2,0:T(8,128)(2,1)} %param.8) | data formatting | bytes 1146880 | tf_op args[0]
  2.0 97.5 %window.1 = bf16[2,64,2560]{2,1,0:T(8,128)(2,1)} custom-call(bf16[2,8,28,640]{3,2,1,0:T(8,128)(2,1)} %copy.9.pix, f32[640]{0:T(1024)} %g1.1, f32[640]{0:T(1024)} %s1_.1, bf16[9,40,640]{2,1,0:T(8,128)(2,1)} %bitcast.9, bf16[40,2560]{1,0:T(8,128)(2,1)} %pr.1, f32[2560]{0:T(1024)} %g2.1, f32[2560]{0:T(1024)} %s2_.1, bf16[9,20,2560]{2,1,0:T(8,128)(2,1)} %bitcast.8), custom_call_target="tpu_custom_call" | custom-call | flops 8000000000 | bytes 10000000 | tf_op jit(solution)/shard_map/window/pallas_call | solution.py:684
  99.5 2.3 %copy.13 = bf16[2,4,14,2560]{3,1,2,0:T(4,128)(2,1)} copy(bf16[2,4,14,2560]{3,2,1,0:T(8,128)(2,1)} %bitcast.7) | data formatting | bytes 1146880
